TPU v7x, 32 devices: a whole 2x2x4 slice. The times are simulated.
32 devices in a mesh: row: 8 (over z, y), col: 4 (over x, core).
Axes of the slice: x: 2, y: 2, z: 4, core: 2. Of those that a mesh axis runs over, the one named last changes fastest.
Arguments:
- rep_a: bfloat16 [4096, 512], P(('row', 'col')), may hold values from -100 to 100
- val_a: bfloat16 [4096, 512], P(('row', 'col')), may hold values from -6 to 6
- rep_b: bfloat16 [4096, 512], P(('row', 'col')), may hold values from -18 to 18
- val_b: bfloat16 [4096, 512], P(('row', 'col')), may hold values from -6 to 6
Outputs:
- mixed_a: float32 [4096, 512], P(('row', 'col'))
- mixed_b: float32 [4096, 512], P(('row', 'col'))
All inputs are finite; a program needn't handle non-finite values.
Results may differ from a plain program's by a relative error of at most 0.0015.
Values may be sent and summed in bfloat16 or wider, within the bound.
A program may use at most 64 MiB of HBM per device.

v0:
```python
import math

import jax
import jax.numpy as jnp
from jax import lax
from jax.sharding import PartitionSpec as P

HEADS = 4
HEAD = 128


def on_device(rep_a, val_a, rep_b, val_b):
    full_a, values_a = (
        lax.all_gather(rep_a, "col", axis=0, tiled=True),
        lax.all_gather(val_a, "col", axis=0, tiled=True),
    )
    full_b, values_b = (
        lax.all_gather(rep_b, "row", axis=0, tiled=True),
        lax.all_gather(val_b, "row", axis=0, tiled=True),
    )
    count_a = full_a.shape[0]
    count_b = full_b.shape[0]
    span_rows = math.gcd(512, count_a)
    blocks = count_a // span_rows
    query_blocks = full_a.reshape(blocks, span_rows, HEADS, HEAD)
    value_blocks = values_a.reshape(blocks, span_rows, HEADS, HEAD)
    key_heads = full_b.reshape(count_b, HEADS, HEAD)
    value_heads = values_b.reshape(count_b, HEADS, HEAD)
    inv_root = HEAD ** (-0.5)

    def make_logits(queries):
        return (
            jnp.einsum("qhd,khd->hqk", queries, key_heads, preferred_element_type=jnp.float32)
            * inv_root
        )

    lowest = jnp.full((HEADS, count_b), -jnp.inf, jnp.float32)

    def first_pass(col_peak, queries):
        logits = make_logits(queries)
        return (jnp.maximum(col_peak, jnp.max(logits, axis=1)), jnp.max(logits, axis=2))

    col_peak, row_peak = lax.scan(first_pass, lowest, query_blocks)

    def fetch_logits(queries):
        return make_logits(queries)

    row_peak = lax.pmax(row_peak, "col")
    col_peak = lax.pmax(col_peak, "row")
    positions = jnp.arange(blocks, dtype=jnp.int32)

    def row_terms(logits, peak_rows):
        weights = jnp.exp(logits - peak_rows[:, :, None])
        weighted = jnp.einsum(
            "hqk,khd->qhd",
            weights.astype(jnp.bfloat16),
            value_heads,
            preferred_element_type=jnp.float32,
        )
        return (weighted, jnp.sum(weights, axis=2))

    def col_terms(logits, block_values):
        weights = jnp.exp(logits - col_peak[:, None, :])
        weighted = jnp.einsum(
            "hqk,qhd->khd",
            weights.astype(jnp.bfloat16),
            block_values,
            preferred_element_type=jnp.float32,
        )
        return (weighted, jnp.sum(weights, axis=1))

    zero_weighted = jnp.zeros((count_b, HEADS, HEAD), jnp.float32)
    zero_sums = jnp.zeros((HEADS, count_b), jnp.float32)

    def second_pass(totals, inputs):
        position, queries, block_values, peak_rows = inputs
        logits = fetch_logits(queries)
        row_outputs = row_terms(logits, peak_rows)
        col_weighted, col_sums = col_terms(logits, block_values)
        return ((totals[0] + col_weighted, totals[1] + col_sums), row_outputs)

    (col_weighted, col_sums), (row_weighted, row_sums) = lax.scan(
        second_pass, (zero_weighted, zero_sums), (positions, query_blocks, value_blocks, row_peak)
    )
    weighted = row_weighted
    sums = row_sums
    weighted = weighted.reshape(count_a, HEADS * HEAD)
    sums = jnp.transpose(sums, (0, 2, 1)).reshape(count_a, HEADS)
    whole_sums = lax.psum(sums, "col")
    scaled = (weighted.reshape(count_a, HEADS, HEAD) / whole_sums[:, :, None]).reshape(
        count_a, HEADS * HEAD
    )
    mixed_a = lax.psum_scatter(scaled, "col", scatter_dimension=0, tiled=True)
    weighted = col_weighted
    sums = col_sums
    weighted = weighted.reshape(count_b, HEADS * HEAD)
    sums = sums.T
    whole_sums = lax.psum(sums, "row")
    scaled = (weighted.reshape(count_b, HEADS, HEAD) / whole_sums[:, :, None]).reshape(
        count_b, HEADS * HEAD
    )
    mixed_b = lax.psum_scatter(scaled, "row", scatter_dimension=0, tiled=True)
    return (mixed_a, mixed_b)


def solution(mesh):
    placed = (
        P(("row", "col"), None),
        P(("row", "col"), None),
        P(("row", "col"), None),
        P(("row", "col"), None),
    )
    return jax.shard_map(
        on_device,
        mesh=mesh,
        in_specs=placed,
        out_specs=(P(("row", "col"), None), P(("row", "col"), None)),
        check_vma=False,
    )
```

profile of v0, /device:TPU:0, one launch (start us, length us, event | category | flops | bytes accessed | tf_op | source)
XLA Modules:
  0.0 237.2 jit_solution(8098616366754442055)
XLA Ops:
  7.2 0.0 all-gather.3.cloned.1.call-start
  7.2 1.7 copy.11
  8.9 0.0 all-gather.5.cloned.1.call-start
  8.9 0.7 all-gather.5.cloned.1.call-update
  9.6 0.0 reduce-scatter.3.cloned.1.call-start
  9.7 1.0 copy.10
  10.7 8.6 %all_gather.12 = bf16[512,512]{0,1:T(8,128)(2,1)S(1)} all-gather(bf16[128,512]{0,1:T(8,128)(2,1)S(1)} %copy.10), channel_id=1, replica_groups=mesh['row'=8,'col'=4] {'col'}, dimensions={0}, use_global_device_ids=true | all-gather | bytes 655360 | tf_op jit(solution)/shard_map/all_gather | solution.py:14
  19.3 33.5 %all-gather.3.cloned.1.call-done = bf16[1024,512]{0,1:T(8,128)(2,1)} async-done(((bf16[128,512]{0,1:T(8,128)(2,1)}), bf16[1024,512]{0,1:T(8,128)(2,1)}) %all-gather.3.cloned.1.call-update) | async-done | bytes 1048592 | tf_op jit(solution)/shard_map/all_gather | solution.py:18
  52.9 5.8 %multiply_reduce_fusion = (f32[4,1024]{1,0:T(4,128)S(1)}, f32[4,512]{1,0:T(4,128)S(1)}, f32[4,512,1024]{2,1,0:T(8,128)}) fusion(bf16[512,4,128]{0,2,1:T(8,128)(2,1)S(1)} %bitcast.22, bf16[1024,4,128]{0,2,1:T(8,128)(2,1)} %bitcast.26), kind=kOutput, calls=%fused_computation.6 | convolution fusion | flops 543156224 | bytes 9986048 | tf_op jit(solution)/shard_map/while/body/eval_jaxpr/qhd,khd->hqk/dot_general | solution.py:33
  58.6 6.3 %pmax.14 = f32[4,512]{1,0:T(4,128)S(1)} all-reduce(f32[4,512]{1,0:T(4,128)S(1)} %get-tuple-element.42), channel_id=1, replica_groups=mesh['row'=8,'col'=4] {'col'}, use_global_device_ids=true, to_apply=%region_1.0 | all-reduce | flops 2048 | bytes 16384 | tf_op jit(solution)/shard_map/pmax | solution.py:48
  64.9 34.9 %pmax.15 = f32[4,1024]{1,0:T(4,128)S(1)} all-reduce(f32[4,1024]{1,0:T(4,128)S(1)} %get-tuple-element.30), channel_id=1, replica_groups=mesh['row'=8,'col'=4] {'row'}, use_global_device_ids=true, to_apply=%region_6.7 | all-reduce | flops 4096 | bytes 32768 | tf_op jit(solution)/shard_map/pmax | solution.py:49
  99.8 5.2 %fusion.2 = (f32[4,1024]{1,0:T(4,128)S(1)}, f32[4,512]{1,0:T(4,128)S(1)}) fusion(f32[4,512,1024]{2,1,0:T(8,128)} %get-tuple-element.43, f32[4,1024]{1,0:T(4,128)S(1)} %pmax.15, f32[4,512]{1,0:T(4,128)S(1)} %pmax.14), kind=kLoop, calls=%fused_computation.4 | loop fusion | flops 10479616 | bytes 8437760 | tf_op jit(solution)/shard_map/while/body/eval_jaxpr/reduce_sum | solution.py:70
  104.9 5.8 %psum.14 = f32[512,4]{0,1:T(4,128)S(1)} all-reduce(f32[512,4]{0,1:T(4,128)S(1)} %bitcast.29), channel_id=1, replica_groups=mesh['row'=8,'col'=4] {'col'}, use_global_device_ids=true, to_apply=%region_3.4 | all-reduce | flops 2048 | bytes 16384 | tf_op jit(solution)/shard_map/psum | solution.py:89
  110.7 0.0 all-gather.5.cloned.1.call-done
  110.8 1.5 copy.14
  112.3 4.5 %fusion.17 = f32[512,4,128]{0,2,1:T(8,128)S(1)} fusion(bf16[1024,4,128]{0,2,1:T(8,128)(2,1)S(1)} %bitcast.24, f32[4,512,1024]{2,1,0:T(8,128)} %get-tuple-element.43, f32[4,512]{1,0:T(4,128)S(1)} %pmax.14, f32[512,4]{0,1:T(4,128)S(1)} %psum.14), kind=kOutput, calls=%fused_computation.16 | convolution fusion | flops 543424512 | bytes 10502144 | tf_op jit(solution)/shard_map/while/body/eval_jaxpr/hqk,khd->qhd/dot_general | solution.py:54
  116.8 1.4 copy.15
  118.2 0.0 reduce-scatter.5.cloned.1.call-start
  118.3 7.4 %all_gather.15 = bf16[512,512]{1,0:T(8,128)(2,1)S(1)} all-gather(bf16[128,512]{1,0:T(8,128)(2,1)S(1)} %copy-done), channel_id=1, replica_groups=mesh['row'=8,'col'=4] {'col'}, dimensions={0}, use_global_device_ids=true | all-gather | bytes 655360 | tf_op jit(solution)/shard_map/all_gather | solution.py:15
  125.7 0.2 copy.16
  125.9 33.0 %psum.15 = f32[1024,4]{0,1:T(4,128)S(1)} all-reduce(f32[1024,4]{0,1:T(4,128)S(1)} %bitcast.28), channel_id=1, replica_groups=mesh['row'=8,'col'=4] {'row'}, use_global_device_ids=true, to_apply=%region_8.9 | all-reduce | flops 4096 | bytes 32768 | tf_op jit(solution)/shard_map/psum | solution.py:98
  158.9 5.1 %bitcast_divide_fusion = f32[1024,4,128]{0,2,1:T(8,128)S(1)} fusion(bf16[512,4,128]{0,2,1:T(8,128)(2,1)S(1)} %bitcast.27, f32[4,512,1024]{2,1,0:T(8,128)} %get-tuple-element.43, f32[4,1024]{1,0:T(4,128)S(1)} %pmax.15, f32[1024,4]{0,1:T(4,128)S(1)} %psum.15), kind=kOutput, calls=%fused_computation.14 | convolution fusion | flops 543686656 | bytes 11042816 | tf_op jit(solution)/shard_map/while/body/eval_jaxpr/hqk,qhd->khd/dot_general | solution.py:64
  164.0 1.9 copy.17
  165.9 64.8 %reduce-scatter.5.cloned.1.call-done = f32[128,512]{1,0:T(8,128)} async-done(((f32[1024,512]{1,0:T(8,128)}), f32[128,512]{1,0:T(8,128)}) %reduce-scatter.5.cloned.1.call-update) | async-done | bytes 262160 | tf_op jit(solution)/shard_map/reduce_scatter | solution.py:102
  (6 shorter events, 0.1 us)
Async XLA Ops:
  7.2 45.7 %all-gather.3.cloned.1.call-start = ((), (), s32[]{:S(2)}) async-start(), calls=%async_computation.2 | async-start | bytes 1179648 | tf_op jit(solution)/shard_map/all_gather | solution.py:18
  8.9 101.9 %all-gather.5.cloned.1.call-start = ((), (), s32[]{:S(2)}) async-start(), calls=%async_computation.3 | async-start | bytes 1179648 | tf_op jit(solution)/shard_map/all_gather | solution.py:19
  9.6 156.3 %reduce-scatter.3.cloned.1.call-start = ((), (), s32[]{:S(2)}) async-start(), calls=%async_computation.4 | async-start | bytes 1310720 | tf_op jit(solution)/shard_map/reduce_scatter | solution.py:93
  112.2 6.0 %copy-start = (bf16[128,512]{1,0:T(8,128)(2,1)S(1)}, bf16[128,512]{1,0:T(8,128)(2,1)}, u32[]{:S(2)}) copy-start(bf16[128,512]{1,0:T(8,128)(2,1)} %param.5) | copy-start | bytes 393220
  118.2 112.5 %reduce-scatter.5.cloned.1.call-start = ((), (), s32[]{:S(2)}) async-start(), calls=%async_computation.5 | async-start | bytes 2359296 | tf_op jit(solution)/shard_map/reduce_scatter | solution.py:102
Sparse Core Ops, SparseCore 0:
  10.6 42.2 all-gather.2
  55.0 39.2 all-gather.4
  118.3 22.3 reduce-scatter.2
  166.0 64.6 reduce-scatter.4
where the time goes:
time: 238 us; the launch traced here: 237 us
  waiting for transfers between devices  99.1 us (42%)
  blocking collectives  95.9 us (40%)
  matrix products  15.4 us (6%)
  between operations  13.8 us (6%)
  local copies, waits for them, and re-layouts  7.68 us (3%)
  other arithmetic  5.16 us (2%)
    reduce_scatter x1, waiting for transfers between devices, on_device(): mixed_b = lax.psum_scatter(scaled, 'row', scatter_dimension=0, tiled=True)  64.8 us
    pmax x1, blocking collectives, on_device(): col_peak = lax.pmax(col_peak, 'row')  34.9 us
    all_gather x1, waiting for transfers between devices, on_device(): lax.all_gather(rep_b, 'row', axis=0, tiled=True)  33.5 us
    psum x1, blocking collectives, on_device(): whole_sums = lax.psum(sums, 'row')  33 us
    all_gather x1, blocking collectives, on_device(): lax.all_gather(rep_a, 'col', axis=0, tiled=True)  8.62 us
    all_gather x1, blocking collectives, on_device(): lax.all_gather(val_a, 'col', axis=0, tiled=True)  7.41 us
    pmax x1, blocking collectives, on_device(): row_peak = lax.pmax(row_peak, 'col')  6.28 us
    psum x1, blocking collectives, on_device(): whole_sums = lax.psum(sums, 'col')  5.77 us
  transfers between devices with their start and end apart: 4, of which 2 were waited for; matrix products, arithmetic and copies ran while one was open for 8% of the time, Pallas kernels for 0%

commit v1 on v0

v1 whole, which is shorter than its diff:
```python
import functools

import jax
import jax.numpy as jnp
from jax import lax
from jax.experimental import pallas as pl
from jax.experimental.pallas import tpu as pltpu
from jax.sharding import PartitionSpec as P

HEADS = 4
HEAD = 128
STATS = 8
MESH = pl.DeviceIdType.MESH


def kernel(
    rows, cols,
    rep_a, val_a, rep_b, val_b, out_a, out_b,
    cut_a, cut_b, in_a, in_b, scores, peak_b,
    part_a, got_a, part_b, mate_b, got_b, done_a, done_b,
    cut_a_send, cut_b_send, a_recv, b_recv, a_send, b_send, mate_send,
    part_a_send, got_a_recv, mate_b_send, mate_b_recv, part_b_send, got_b_recv,
    done_a_send, done_b_send, done_a_recv, done_b_recv,
):
    Q, K = rows // HEADS, cols // 2
    n_a, n_b = rep_a.shape[0], rep_b.shape[0]
    row, col = lax.axis_index("row"), lax.axis_index("col")
    p, q = row // Q, row % Q
    k, c = col // 2, col % 2
    s = q * 2 + c
    inv_root = HEAD ** -0.5

    def head_at(d):
        return (p + d) % HEADS

    def at_head(d):
        return (head_at(d) * Q + q, col)

    def at_k(d):
        return (row, (k + d) % K * 2 + c)

    def at_q(d):
        return (p * Q + (q + d) % Q, col)

    mate = (row, k * 2 + 1 - c)

    def remote(src, dst, send, recv, device):
        return pltpu.make_async_remote_copy(
            src_ref=src, dst_ref=dst, send_sem=send, recv_sem=recv,
            device_id=device, device_id_type=MESH,
        )

    barrier = pltpu.get_barrier_semaphore()
    peers = [at_head(d) for d in range(1, HEADS)] + [at_k(d) for d in range(1, K)]
    peers += [at_q(d) for d in range(1, Q)] + [mate]
    for peer in peers:
        pl.semaphore_signal(barrier, inc=1, device_id=peer, device_id_type=MESH)

    for h in range(HEADS):
        lanes = slice(h * HEAD, (h + 1) * HEAD)
        cut_b[h, 0] = rep_b[:, lanes]
        cut_b[h, 1] = val_b[:, lanes]
        cut_a[h, 0] = rep_a[:, lanes]
        cut_a[h, 1] = val_a[:, lanes]
    in_b[s, p] = cut_b[p]
    in_a[k, p] = cut_a[p]
    peak_b[...] = jnp.full_like(peak_b, -jnp.inf)
    pl.semaphore_wait(barrier, len(peers))

    def cut_b_copy(d):
        h = head_at(d)
        return remote(cut_b.at[h], in_b.at[s, p], cut_b_send.at[d], b_recv.at[s, p], at_head(d))

    def cut_a_copy(d):
        h = head_at(d)
        return remote(cut_a.at[h], in_a.at[k, p], cut_a_send.at[d], a_recv.at[k, p], at_head(d))

    def a_copy(d, e):
        piece = in_a.at[k, head_at(e)]
        return remote(piece, piece, a_send.at[d, e], a_recv.at[k, head_at(e)], at_k(d))

    def b_copy(d, e):
        piece = in_b.at[s, head_at(e)]
        return remote(piece, piece, b_send.at[d, e], b_recv.at[s, head_at(e)], at_q(d))

    def mate_copy(d, e):
        r = (q + d) % Q * 2 + c
        piece = in_b.at[r, head_at(e)]
        return remote(piece, piece, mate_send.at[d, e], b_recv.at[r, head_at(e)], mate)

    def wait_b(r, e, device):
        piece = in_b.at[r, head_at(e)]
        remote(piece, piece, mate_send.at[0, 0], b_recv.at[r, head_at(e)], device).wait_recv()

    def wait_a(r, e, device):
        piece = in_a.at[r, head_at(e)]
        remote(piece, piece, mate_send.at[0, 0], a_recv.at[r, head_at(e)], device).wait_recv()

    for d in range(1, HEADS):
        cut_b_copy(d).start()
    for d in range(1, HEADS):
        cut_a_copy(d).start()
    for e in range(HEADS):
        if e:
            wait_b(s, e, at_head(e))
        for d in range(1, Q):
            b_copy(d, e).start()
        mate_copy(0, e).start()
        if e == 0:
            for d in range(1, K):
                a_copy(d, 0).start()
    for e in range(HEADS):
        for d in range(1, Q):
            wait_b((q + d) % Q * 2 + c, e, at_q(d))
            mate_copy(d, e).start()
    for e in range(HEADS):
        for d in range(Q):
            wait_b((q + d) % Q * 2 + 1 - c, e, mate)

    width = HEADS * n_b
    high = HEADS * n_a

    def row_block(kk, pp):
        start = pl.multiple_of((kk * HEADS + pp) * n_a, n_a)
        queries = in_a[kk, pp, 0]
        peak = jnp.full((n_a, 1), -jnp.inf, jnp.float32)
        for r in range(2 * Q):
            keys = in_b[r, :, 0].reshape(width, HEAD)
            logits = lax.dot_general(
                queries, keys, (((1,), (1,)), ((), ())), preferred_element_type=jnp.float32
            ) * inv_root
            scores[r, pl.ds(start, n_a), :] = logits
            peak_b[r] = jnp.maximum(peak_b[r], jnp.max(logits, axis=0, keepdims=True))
            peak = jnp.maximum(peak, jnp.max(logits, axis=1, keepdims=True))
        total = jnp.zeros((n_a, 1), jnp.float32)
        num = jnp.zeros((n_a, HEAD), jnp.float32)
        for r in range(2 * Q):
            values = in_b[r, :, 1].reshape(width, HEAD)
            weights = jnp.exp(scores[r, pl.ds(start, n_a), :] - peak)
            total += jnp.sum(weights, axis=1, keepdims=True)
            num += jnp.dot(
                weights.astype(jnp.bfloat16), values, preferred_element_type=jnp.float32
            )
        lane = lax.broadcasted_iota(jnp.int32, (n_a, HEAD), 1)
        stats = jnp.where(lane == 0, peak, total)
        part_a[kk, pp, 0:HEAD] = num.T
        part_a[kk, pp, HEAD:HEAD + STATS] = stats.T[0:STATS]

    def part_a_copy(d, e):
        there = (k + d) % K
        h = head_at(e)
        return remote(
            part_a.at[there, h], got_a.at[k, h], part_a_send.at[d, e], got_a_recv.at[k, h], at_k(d)
        )

    def other_rows(e):
        for d in range(1, K):
            kk = (k + d) % K
            wait_a(kk, e, at_k(d))
            row_block(kk, head_at(e))
            part_a_copy(d, e).start()

    row_block(k, p)

    @pl.loop(1, HEADS)
    def _(e):
        wait_a(k, e, at_head(e))
        for d in range(1, K):
            a_copy(d, e).start()
        row_block(k, head_at(e))
        other_rows(e - 1)

    other_rows(HEADS - 1)

    values_t = in_a[:, :, 1].reshape(K * high, HEAD).T

    def col_block(r):
        peak = peak_b[r]
        weights = jnp.exp(scores[r] - peak)
        total = jnp.sum(weights, axis=0, keepdims=True)
        num = jnp.dot(values_t, weights.astype(jnp.bfloat16), preferred_element_type=jnp.float32)
        sub = lax.broadcasted_iota(jnp.int32, (STATS, width), 0)
        stats = jnp.where(sub == 0, peak, total)
        for h in range(HEADS):
            part_b[r, h, 0:HEAD] = num[:, h * n_b:(h + 1) * n_b]
            part_b[r, h, HEAD:HEAD + STATS] = stats[:, h * n_b:(h + 1) * n_b]

    def mate_b_copy(d):
        qq = (q + d) % Q
        return remote(
            part_b.at[qq * 2 + 1 - c], mate_b.at[qq], mate_b_send.at[d], mate_b_recv.at[qq], mate
        )

    def part_b_copy(d, e):
        there = (q + d) % Q * 2 + c
        h = head_at(e)
        return remote(
            part_b.at[there, h], got_b.at[q, h], part_b_send.at[d, e], got_b_recv.at[q, h], at_q(d)
        )

    order = [d % Q for d in range(1, Q + 1)]
    for d in order:
        col_block((q + d) % Q * 2 + 1 - c)
        mate_b_copy(d).start()
    for d in order:
        col_block((q + d) % Q * 2 + c)

    def merged(parts):
        peak = functools.reduce(jnp.maximum, [x[HEAD:HEAD + 1] for x in parts])
        scales = [jnp.exp(x[HEAD:HEAD + 1] - peak) for x in parts]
        num = sum(x[0:HEAD] * w for x, w in zip(parts, scales))
        total = sum(x[HEAD + 1:HEAD + 2] * w for x, w in zip(parts, scales))
        return num, total, peak

    for d in order:
        qq = (q + d) % Q
        mate_b_copy(d).wait_recv()
        for e in range(HEADS):
            h = head_at(e)
            num, total, peak = merged([part_b[qq * 2 + c, h], mate_b[qq, h]])
            part_b[qq * 2 + c, h, 0:HEAD] = num
            part_b[qq * 2 + c, h, HEAD:HEAD + 1] = peak
            part_b[qq * 2 + c, h, HEAD + 1:HEAD + 2] = total
            if d:
                part_b_copy(d, e).start()

    own_lanes = pl.ds(pl.multiple_of(p * HEAD, HEAD), HEAD)

    def done_copy(e, done, out, send, recv):
        return remote(done.at[head_at(e)], out.at[:, own_lanes], send.at[e], recv.at[p], at_head(e))

    def wait_done(e, done, out, send, recv):
        lanes = pl.ds(pl.multiple_of(head_at(e) * HEAD, HEAD), HEAD)
        remote(
            done.at[head_at(e)], out.at[:, lanes], send.at[e], recv.at[head_at(e)], at_head(e)
        ).wait_recv()

    def finish(e, parts, done, out, send, recv):
        num, total, _ = merged(parts)
        result = (num / total).T
        if e:
            done[head_at(e)] = result
            done_copy(e, done, out, send, recv).start()
        else:
            out[:, own_lanes] = result

    last = [d % HEADS for d in range(1, HEADS + 1)]
    for e in last:
        h = head_at(e)
        parts = [part_a[k, h]]
        for d in range(1, K):
            kk = (k + d) % K
            remote(
                part_a.at[kk, h], got_a.at[kk, h], part_a_send.at[d, e], got_a_recv.at[kk, h],
                at_k(d),
            ).wait_recv()
            parts.append(got_a[kk, h])
        finish(e, parts, done_a, out_a, done_a_send, done_a_recv)
    for e in last:
        h = head_at(e)
        parts = [part_b[s, h]]
        for d in range(1, Q):
            qq = (q + d) % Q
            remote(
                part_b.at[qq * 2 + c, h], got_b.at[qq, h], part_b_send.at[d, e],
                got_b_recv.at[qq, h], at_q(d),
            ).wait_recv()
            parts.append(got_b[qq, h])
        finish(e, parts, done_b, out_b, done_b_send, done_b_recv)

    for d in range(1, HEADS):
        cut_b_copy(d).wait_send()
        cut_a_copy(d).wait_send()
    for e in range(HEADS):
        for d in range(1, K):
            a_copy(d, e).wait_send()
            part_a_copy(d, e).wait_send()
        for d in range(Q):
            if d:
                b_copy(d, e).wait_send()
                part_b_copy(d, e).wait_send()
            mate_copy(d, e).wait_send()
    for d in range(Q):
        mate_b_copy(d).wait_send()
    for e in range(1, HEADS):
        done_copy(e, done_a, out_a, done_a_send, done_a_recv).wait_send()
        done_copy(e, done_b, out_b, done_b_send, done_b_recv).wait_send()
    for e in range(1, HEADS):
        wait_done(e, done_a, out_a, done_a_send, done_a_recv)
        wait_done(e, done_b, out_b, done_b_send, done_b_recv)


def on_device(rows, cols, rep_a, val_a, rep_b, val_b):
    Q, K = rows // HEADS, cols // 2
    n_a, n_b = rep_a.shape[0], rep_b.shape[0]
    f32, bf16 = jnp.float32, jnp.bfloat16
    tall = HEAD + STATS
    dma = pltpu.SemaphoreType.DMA
    vmem = pl.BlockSpec(memory_space=pltpu.VMEM)
    tile = K * HEADS * n_a * 2 * Q * HEADS * n_b
    return pl.pallas_call(
        functools.partial(kernel, rows, cols),
        out_shape=(
            jax.ShapeDtypeStruct(rep_a.shape, f32),
            jax.ShapeDtypeStruct(rep_b.shape, f32),
        ),
        in_specs=[vmem] * 4,
        out_specs=(vmem, vmem),
        scratch_shapes=[
            pltpu.VMEM((HEADS, 2, n_a, HEAD), bf16),
            pltpu.VMEM((HEADS, 2, n_b, HEAD), bf16),
            pltpu.VMEM((K, HEADS, 2, n_a, HEAD), bf16),
            pltpu.VMEM((2 * Q, HEADS, 2, n_b, HEAD), bf16),
            pltpu.VMEM((2 * Q, K * HEADS * n_a, HEADS * n_b), f32),
            pltpu.VMEM((2 * Q, 1, HEADS * n_b), f32),
            pltpu.VMEM((K, HEADS, tall, n_a), f32),
            pltpu.VMEM((K, HEADS, tall, n_a), f32),
            pltpu.VMEM((2 * Q, HEADS, tall, n_b), f32),
            pltpu.VMEM((Q, HEADS, tall, n_b), f32),
            pltpu.VMEM((Q, HEADS, tall, n_b), f32),
            pltpu.VMEM((HEADS, n_a, HEAD), f32),
            pltpu.VMEM((HEADS, n_b, HEAD), f32),
            dma((HEADS,)), dma((HEADS,)),
            dma((K, HEADS)), dma((2 * Q, HEADS)),
            dma((K, HEADS)), dma((Q, HEADS)), dma((Q, HEADS)),
            dma((K, HEADS)), dma((K, HEADS)),
            dma((Q,)), dma((Q,)),
            dma((Q, HEADS)), dma((Q, HEADS)),
            dma((HEADS,)), dma((HEADS,)), dma((HEADS,)), dma((HEADS,)),
        ],
        compiler_params=pltpu.CompilerParams(
            collective_id=0, has_side_effects=True, vmem_limit_bytes=48 * 1024 * 1024
        ),
        cost_estimate=pl.CostEstimate(
            flops=6 * tile * HEAD, bytes_accessed=6 * 1024 * (n_a + n_b), transcendentals=2 * tile
        ),
    )(rep_a, val_a, rep_b, val_b)


def solution(mesh):
    rows, cols = mesh.shape["row"], mesh.shape["col"]
    placed = P(("row", "col"), None)
    return jax.shard_map(
        functools.partial(on_device, rows, cols),
        mesh=mesh,
        in_specs=(placed,) * 4,
        out_specs=(placed, placed),
        check_vma=False,
    )
```

time: 238 us -> 52.3 us (0.22)
  waiting for transfers between devices: 99.1 us -> 0 us
  blocking collectives: 95.9 us -> 0 us
  Pallas kernels: 0 us -> 46.5 us
  matrix products: 15.4 us -> 0 us
  between operations: 13.8 us -> 0.65 us
  other arithmetic: 5.16 us -> 0 us
  local copies, waits for them, and re-layouts: 7.68 us -> 5.02 us
    reduce_scatter x2 -> x0, waiting for transfers between devices: 64.8 us -> none  [the longest x1 64.8 us: on_device(): mixed_b = lax.psum_scatter(scaled, 'row', scatter_dimension=0, tiled=True)]
    pallas_call x0 -> x1, Pallas kernels: none -> 46.5 us  [on_device(): pl.pallas_call(functools.partial(kernel, rows, cols), out_shape=(jax.Shap...]
    pmax x2 -> x0, blocking collectives: 41.1 us -> none  [the longest x1 34.9 us: on_device(): col_peak = lax.pmax(col_peak, 'row')]
    psum x2 -> x0, blocking collectives: 38.7 us -> none  [the longest x1 33 us: on_device(): whole_sums = lax.psum(sums, 'row')]
    all_gather x2 -> x0, waiting for transfers between devices: 33.6 us -> none  [the longest x1 33.5 us: on_device(): lax.all_gather(rep_b, 'row', axis=0, tiled=True)]
    all_gather x2 -> x0, blocking collectives: 16 us -> none  [the longest x1 8.62 us: on_device(): lax.all_gather(rep_a, 'col', axis=0, tiled=True)]
    dot_general x3 -> x0, matrix products: 15.4 us -> none  [the longest x1 5.77 us: make_logits(): jnp.einsum('qhd,khd->hqk', queries, key_heads, preferred_element_type=jnp...]
    reduce_sum x1 -> x0, other arithmetic: 5.16 us -> none  [col_terms(): return (weighted, jnp.sum(weights, axis=1))]
  transfers between devices with their start and end apart: 4 -> 0, of which waited for: 2 -> 0; matrix products, arithmetic and copies ran while one was open for 8% -> 0% of each run, Pallas kernels for 0% -> 0%
where the time goes in v1:
time: 52.3 us; the launch traced here: 52.1 us
  Pallas kernels  46.5 us (89%)
  local copies, waits for them, and re-layouts  5.02 us (10%)
  between operations  0.65 us (1%)
    pallas_call x1, Pallas kernels, on_device(): pl.pallas_call(functools.partial(kernel, rows, cols), out_shape=(jax.Shap...  46.5 us
    unnamed x10, local copies, waits for them, and re-layouts  5.02 us

profile of v1, /device:TPU:0, one launch (start us, length us, event | category | flops | bytes accessed | tf_op | source)
XLA Modules:
  0.0 52.1 jit_solution(1029080910026390503)
XLA Ops:
  0.6 0.0 copy-start
  0.6 0.9 %copy-done = bf16[128,512]{1,0:T(8,128)(2,1)S(1)} copy-done((bf16[128,512]{1,0:T(8,128)(2,1)S(1)}, bf16[128,512]{1,0:T(8,128)(2,1)}, u32[]{:S(2)}) %copy-start) | copy-done | bytes 131096
  1.5 0.0 copy-start.1
  1.5 0.9 %copy-done.1 = bf16[128,512]{1,0:T(8,128)(2,1)S(1)} copy-done((bf16[128,512]{1,0:T(8,128)(2,1)S(1)}, bf16[128,512]{1,0:T(8,128)(2,1)}, u32[]{:S(2)}) %copy-start.1) | copy-done | bytes 131096
  2.4 0.0 copy-start.2
  2.4 0.9 %copy-done.2 = bf16[128,512]{1,0:T(8,128)(2,1)S(1)} copy-done((bf16[128,512]{1,0:T(8,128)(2,1)S(1)}, bf16[128,512]{1,0:T(8,128)(2,1)}, u32[]{:S(2)}) %copy-start.2) | copy-done | bytes 131096
  3.3 0.0 copy-start.3
  3.3 0.9 %copy-done.3 = bf16[128,512]{1,0:T(8,128)(2,1)S(1)} copy-done((bf16[128,512]{1,0:T(8,128)(2,1)S(1)}, bf16[128,512]{1,0:T(8,128)(2,1)}, u32[]{:S(2)}) %copy-start.3) | copy-done | bytes 131096
  4.2 46.5 %shard_map.59 = (f32[128,512]{1,0:T(8,128)S(1)}, f32[128,512]{1,0:T(8,128)S(1)}) custom-call(bf16[128,512]{1,0:T(8,128)(2,1)S(1)} %copy-done, bf16[128,512]{1,0:T(8,128)(2,1)S(1)} %copy-done.1, bf16[128,512]{1,0:T(8,128)(2,1)S(1)} %copy-done.2, bf16[128,512]{1,0:T(8,128)(2,1)S(1)} %copy-done.3), custom_call_target="tpu_custom_call" | custom-call | flops 1610612736 | bytes 1572864 | tf_op jit(solution)/shard_map/pallas_call | solution.py:301
  50.7 0.7 %copy.8 = f32[128,512]{1,0:T(8,128)} copy(f32[128,512]{1,0:T(8,128)S(1)} %get-tuple-element.4) | data formatting | bytes 524288
  51.4 0.7 %copy.9 = f32[128,512]{1,0:T(8,128)} copy(f32[128,512]{1,0:T(8,128)S(1)} %get-tuple-element.5) | data formatting | bytes 524288
Async XLA Ops:
  0.6 0.9 %copy-start = (bf16[128,512]{1,0:T(8,128)(2,1)S(1)}, bf16[128,512]{1,0:T(8,128)(2,1)}, u32[]{:S(2)}) copy-start(bf16[128,512]{1,0:T(8,128)(2,1)} %rep_a.1) | copy-start | bytes 393220
  1.5 0.9 %copy-start.1 = (bf16[128,512]{1,0:T(8,128)(2,1)S(1)}, bf16[128,512]{1,0:T(8,128)(2,1)}, u32[]{:S(2)}) copy-start(bf16[128,512]{1,0:T(8,128)(2,1)} %val_a.1) | copy-start | bytes 393220
  2.4 0.9 %copy-start.2 = (bf16[128,512]{1,0:T(8,128)(2,1)S(1)}, bf16[128,512]{1,0:T(8,128)(2,1)}, u32[]{:S(2)}) copy-start(bf16[128,512]{1,0:T(8,128)(2,1)} %rep_b.1) | copy-start | bytes 393220
  3.3 0.9 %copy-start.3 = (bf16[128,512]{1,0:T(8,128)(2,1)S(1)}, bf16[128,512]{1,0:T(8,128)(2,1)}, u32[]{:S(2)}) copy-start(bf16[128,512]{1,0:T(8,128)(2,1)} %val_b.1) | copy-start | bytes 393220

commit v2 on v1

--- a/solution.py
+++ b/solution.py
@@ -1,4 +1,5 @@
 import functools
+import math
 
 import jax
 import jax.numpy as jnp
@@ -16,9 +17,9 @@
 def kernel(
     rows, cols,
     rep_a, val_a, rep_b, val_b, out_a, out_b,
-    cut_a, cut_b, in_a, in_b, scores, peak_b,
+    in_a, in_b, keys_t, scores, peak_b,
     part_a, got_a, part_b, mate_b, got_b, done_a, done_b,
-    cut_a_send, cut_b_send, a_recv, b_recv, a_send, b_send, mate_send,
+    own, cut_a_send, cut_b_send, a_recv, b_recv, a_send, b_send, mate_send,
     part_a_send, got_a_recv, mate_b_send, mate_b_recv, part_b_send, got_b_recv,
     done_a_send, done_b_send, done_a_recv, done_b_recv,
 ):
@@ -28,7 +29,7 @@
     p, q = row // Q, row % Q
     k, c = col // 2, col % 2
     s = q * 2 + c
-    inv_root = HEAD ** -0.5
+    to_log2 = HEAD ** -0.5 * math.log2(math.e)
 
     def head_at(d):
         return (p + d) % HEADS
@@ -56,27 +57,36 @@
     for peer in peers:
         pl.semaphore_signal(barrier, inc=1, device_id=peer, device_id_type=MESH)
 
-    for h in range(HEADS):
-        lanes = slice(h * HEAD, (h + 1) * HEAD)
-        cut_b[h, 0] = rep_b[:, lanes]
-        cut_b[h, 1] = val_b[:, lanes]
-        cut_a[h, 0] = rep_a[:, lanes]
-        cut_a[h, 1] = val_a[:, lanes]
-    in_b[s, p] = cut_b[p]
-    in_a[k, p] = cut_a[p]
+    def head_lanes(h):
+        return pl.ds(pl.multiple_of(h * HEAD, HEAD), HEAD)
+
+    own_lanes = head_lanes(p)
+    own_copies = [
+        pltpu.make_async_copy(x.at[:, own_lanes], y, own.at[i])
+        for i, (x, y) in enumerate([
+            (rep_b, in_b.at[s, p, 0]), (val_b, in_b.at[s, p, 1]),
+            (rep_a, in_a.at[p, k, 0]), (val_a, in_a.at[p, k, 1]),
+        ])
+    ]
+    for copy in own_copies:
+        copy.start()
     peak_b[...] = jnp.full_like(peak_b, -jnp.inf)
     pl.semaphore_wait(barrier, len(peers))
 
-    def cut_b_copy(d):
-        h = head_at(d)
-        return remote(cut_b.at[h], in_b.at[s, p], cut_b_send.at[d], b_recv.at[s, p], at_head(d))
-
-    def cut_a_copy(d):
-        h = head_at(d)
-        return remote(cut_a.at[h], in_a.at[k, p], cut_a_send.at[d], a_recv.at[k, p], at_head(d))
+    def cut_b_copy(d, i):
+        return remote(
+            (rep_b, val_b)[i].at[:, head_lanes(head_at(d))], in_b.at[s, p, i],
+            cut_b_send.at[d, i], b_recv.at[s, p], at_head(d),
+        )
+
+    def cut_a_copy(d, i):
+        return remote(
+            (rep_a, val_a)[i].at[:, head_lanes(head_at(d))], in_a.at[p, k, i],
+            cut_a_send.at[d, i], a_recv.at[k, p], at_head(d),
+        )
 
     def a_copy(d, e):
-        piece = in_a.at[k, head_at(e)]
+        piece = in_a.at[head_at(e), k]
         return remote(piece, piece, a_send.at[d, e], a_recv.at[k, head_at(e)], at_k(d))
 
     def b_copy(d, e):
@@ -93,13 +103,15 @@
         remote(piece, piece, mate_send.at[0, 0], b_recv.at[r, head_at(e)], device).wait_recv()
 
     def wait_a(r, e, device):
-        piece = in_a.at[r, head_at(e)]
+        piece = in_a.at[head_at(e), r]
         remote(piece, piece, mate_send.at[0, 0], a_recv.at[r, head_at(e)], device).wait_recv()
 
-    for d in range(1, HEADS):
-        cut_b_copy(d).start()
-    for d in range(1, HEADS):
-        cut_a_copy(d).start()
+    for cut in (cut_b_copy, cut_a_copy):
+        for d in range(1, HEADS):
+            for i in range(2):
+                cut(d, i).start()
+    for copy in own_copies:
+        copy.wait()
     for e in range(HEADS):
         if e:
             wait_b(s, e, at_head(e))
@@ -116,35 +128,36 @@
     for e in range(HEADS):
         for d in range(Q):
             wait_b((q + d) % Q * 2 + 1 - c, e, mate)
+    for r in range(2 * Q):
+        keys_t[r] = in_b[r, :, 0].reshape(HEADS * n_b, HEAD).T
 
     width = HEADS * n_b
-    high = HEADS * n_a
-
-    def row_block(kk, pp):
-        start = pl.multiple_of((kk * HEADS + pp) * n_a, n_a)
-        queries = in_a[kk, pp, 0]
-        peak = jnp.full((n_a, 1), -jnp.inf, jnp.float32)
+    span = K * n_a
+
+    def row_block(pp):
+        start = pl.multiple_of(pp * span, span)
+        queries = in_a[pp, :, 0].reshape(span, HEAD)
+        peak = jnp.full((span, 1), -jnp.inf, jnp.float32)
         for r in range(2 * Q):
-            keys = in_b[r, :, 0].reshape(width, HEAD)
-            logits = lax.dot_general(
-                queries, keys, (((1,), (1,)), ((), ())), preferred_element_type=jnp.float32
-            ) * inv_root
-            scores[r, pl.ds(start, n_a), :] = logits
+            logits = jnp.dot(queries, keys_t[r], preferred_element_type=jnp.float32) * to_log2
+            scores[r, pl.ds(start, span), :] = logits
             peak_b[r] = jnp.maximum(peak_b[r], jnp.max(logits, axis=0, keepdims=True))
             peak = jnp.maximum(peak, jnp.max(logits, axis=1, keepdims=True))
-        total = jnp.zeros((n_a, 1), jnp.float32)
-        num = jnp.zeros((n_a, HEAD), jnp.float32)
+        total = jnp.zeros((span, 1), jnp.float32)
+        num = jnp.zeros((span, HEAD), jnp.float32)
         for r in range(2 * Q):
             values = in_b[r, :, 1].reshape(width, HEAD)
-            weights = jnp.exp(scores[r, pl.ds(start, n_a), :] - peak)
+            weights = jnp.exp2(scores[r, pl.ds(start, span), :] - peak)
             total += jnp.sum(weights, axis=1, keepdims=True)
             num += jnp.dot(
                 weights.astype(jnp.bfloat16), values, preferred_element_type=jnp.float32
             )
-        lane = lax.broadcasted_iota(jnp.int32, (n_a, HEAD), 1)
+        lane = lax.broadcasted_iota(jnp.int32, (span, HEAD), 1)
         stats = jnp.where(lane == 0, peak, total)
-        part_a[kk, pp, 0:HEAD] = num.T
-        part_a[kk, pp, HEAD:HEAD + STATS] = stats.T[0:STATS]
+        for kk in range(K):
+            mine = slice(kk * n_a, (kk + 1) * n_a)
+            part_a[kk, pp, 0:HEAD] = num[mine].T
+            part_a[kk, pp, HEAD:HEAD + STATS] = stats[mine].T[0:STATS]
 
     def part_a_copy(d, e):
         there = (k + d) % K
@@ -153,30 +166,27 @@
             part_a.at[there, h], got_a.at[k, h], part_a_send.at[d, e], got_a_recv.at[k, h], at_k(d)
         )
 
-    def other_rows(e):
-        for d in range(1, K):
-            kk = (k + d) % K
-            wait_a(kk, e, at_k(d))
-            row_block(kk, head_at(e))
+    def rows_of(e):
+        for d in range(1, K):
+            wait_a((k + d) % K, e, at_k(d))
+        row_block(head_at(e))
+        for d in range(1, K):
             part_a_copy(d, e).start()
 
-    row_block(k, p)
-
-    @pl.loop(1, HEADS)
+    @pl.loop(0, HEADS - 1)
     def _(e):
-        wait_a(k, e, at_head(e))
-        for d in range(1, K):
-            a_copy(d, e).start()
-        row_block(k, head_at(e))
-        other_rows(e - 1)
-
-    other_rows(HEADS - 1)
-
-    values_t = in_a[:, :, 1].reshape(K * high, HEAD).T
+        wait_a(k, e + 1, at_head(e + 1))
+        for d in range(1, K):
+            a_copy(d, e + 1).start()
+        rows_of(e)
+
+    rows_of(HEADS - 1)
+
+    values_t = in_a[:, :, 1].reshape(HEADS * span, HEAD).T
 
     def col_block(r):
         peak = peak_b[r]
-        weights = jnp.exp(scores[r] - peak)
+        weights = jnp.exp2(scores[r] - peak)
         total = jnp.sum(weights, axis=0, keepdims=True)
         num = jnp.dot(values_t, weights.astype(jnp.bfloat16), preferred_element_type=jnp.float32)
         sub = lax.broadcasted_iota(jnp.int32, (STATS, width), 0)
@@ -199,18 +209,55 @@
         )
 
     order = [d % Q for d in range(1, Q + 1)]
-    for d in order:
-        col_block((q + d) % Q * 2 + 1 - c)
-        mate_b_copy(d).start()
-    for d in order:
-        col_block((q + d) % Q * 2 + c)
 
     def merged(parts):
         peak = functools.reduce(jnp.maximum, [x[HEAD:HEAD + 1] for x in parts])
-        scales = [jnp.exp(x[HEAD:HEAD + 1] - peak) for x in parts]
+        scales = [jnp.exp2(x[HEAD:HEAD + 1] - peak) for x in parts]
         num = sum(x[0:HEAD] * w for x, w in zip(parts, scales))
         total = sum(x[HEAD + 1:HEAD + 2] * w for x, w in zip(parts, scales))
         return num, total, peak
+
+    def done_copy(e, done, out, send, recv):
+        return remote(done.at[head_at(e)], out.at[:, own_lanes], send.at[e], recv.at[p], at_head(e))
+
+    def wait_done(e, done, out, send, recv):
+        remote(
+            done.at[head_at(e)], out.at[:, head_lanes(head_at(e))], send.at[e], recv.at[head_at(e)], at_head(e)
+        ).wait_recv()
+
+    def finish(e, parts, done, out, send, recv):
+        num, total, _ = merged(parts)
+        result = (num / total).T
+        if e:
+            done[head_at(e)] = result
+            done_copy(e, done, out, send, recv).start()
+        else:
+            out[:, own_lanes] = result
+
+    last = [d % HEADS for d in range(1, HEADS + 1)]
+
+    def finish_a(e):
+        h = head_at(e)
+        parts = [part_a[k, h]]
+        for d in range(1, K):
+            kk = (k + d) % K
+            remote(
+                part_a.at[kk, h], got_a.at[kk, h], part_a_send.at[d, e], got_a_recv.at[kk, h],
+                at_k(d),
+            ).wait_recv()
+            parts.append(got_a[kk, h])
+        finish(e, parts, done_a, out_a, done_a_send, done_a_recv)
+
+    blocks = 2 * Q
+    for i in range(blocks):
+        d = order[i % Q]
+        if i < Q:
+            col_block((q + d) % Q * 2 + 1 - c)
+            mate_b_copy(d).start()
+        else:
+            col_block((q + d) % Q * 2 + c)
+        for e in last[i * HEADS // blocks:(i + 1) * HEADS // blocks]:
+            finish_a(e)
 
     for d in order:
         qq = (q + d) % Q
@@ -224,38 +271,6 @@
             if d:
                 part_b_copy(d, e).start()
 
-    own_lanes = pl.ds(pl.multiple_of(p * HEAD, HEAD), HEAD)
-
-    def done_copy(e, done, out, send, recv):
-        return remote(done.at[head_at(e)], out.at[:, own_lanes], send.at[e], recv.at[p], at_head(e))
-
-    def wait_done(e, done, out, send, recv):
-        lanes = pl.ds(pl.multiple_of(head_at(e) * HEAD, HEAD), HEAD)
-        remote(
-            done.at[head_at(e)], out.at[:, lanes], send.at[e], recv.at[head_at(e)], at_head(e)
-        ).wait_recv()
-
-    def finish(e, parts, done, out, send, recv):
-        num, total, _ = merged(parts)
-        result = (num / total).T
-        if e:
-            done[head_at(e)] = result
-            done_copy(e, done, out, send, recv).start()
-        else:
-            out[:, own_lanes] = result
-
-    last = [d % HEADS for d in range(1, HEADS + 1)]
-    for e in last:
-        h = head_at(e)
-        parts = [part_a[k, h]]
-        for d in range(1, K):
-            kk = (k + d) % K
-            remote(
-                part_a.at[kk, h], got_a.at[kk, h], part_a_send.at[d, e], got_a_recv.at[kk, h],
-                at_k(d),
-            ).wait_recv()
-            parts.append(got_a[kk, h])
-        finish(e, parts, done_a, out_a, done_a_send, done_a_recv)
     for e in last:
         h = head_at(e)
         parts = [part_b[s, h]]
@@ -269,8 +284,9 @@
         finish(e, parts, done_b, out_b, done_b_send, done_b_recv)
 
     for d in range(1, HEADS):
-        cut_b_copy(d).wait_send()
-        cut_a_copy(d).wait_send()
+        for i in range(2):
+            cut_b_copy(d, i).wait_send()
+            cut_a_copy(d, i).wait_send()
     for e in range(HEADS):
         for d in range(1, K):
             a_copy(d, e).wait_send()
@@ -297,6 +313,7 @@
     tall = HEAD + STATS
     dma = pltpu.SemaphoreType.DMA
     vmem = pl.BlockSpec(memory_space=pltpu.VMEM)
+    hbm = pl.BlockSpec(memory_space=pltpu.HBM)
     tile = K * HEADS * n_a * 2 * Q * HEADS * n_b
     return pl.pallas_call(
         functools.partial(kernel, rows, cols),
@@ -304,13 +321,12 @@
             jax.ShapeDtypeStruct(rep_a.shape, f32),
             jax.ShapeDtypeStruct(rep_b.shape, f32),
         ),
-        in_specs=[vmem] * 4,
+        in_specs=[hbm] * 4,
         out_specs=(vmem, vmem),
         scratch_shapes=[
-            pltpu.VMEM((HEADS, 2, n_a, HEAD), bf16),
-            pltpu.VMEM((HEADS, 2, n_b, HEAD), bf16),
-            pltpu.VMEM((K, HEADS, 2, n_a, HEAD), bf16),
+            pltpu.VMEM((HEADS, K, 2, n_a, HEAD), bf16),
             pltpu.VMEM((2 * Q, HEADS, 2, n_b, HEAD), bf16),
+            pltpu.VMEM((2 * Q, HEAD, HEADS * n_b), bf16),
             pltpu.VMEM((2 * Q, K * HEADS * n_a, HEADS * n_b), f32),
             pltpu.VMEM((2 * Q, 1, HEADS * n_b), f32),
             pltpu.VMEM((K, HEADS, tall, n_a), f32),
@@ -320,7 +336,7 @@
             pltpu.VMEM((Q, HEADS, tall, n_b), f32),
             pltpu.VMEM((HEADS, n_a, HEAD), f32),
             pltpu.VMEM((HEADS, n_b, HEAD), f32),
-            dma((HEADS,)), dma((HEADS,)),
+            dma((4,)), dma((HEADS, 2)), dma((HEADS, 2)),
             dma((K, HEADS)), dma((2 * Q, HEADS)),
             dma((K, HEADS)), dma((Q, HEADS)), dma((Q, HEADS)),
             dma((K, HEADS)), dma((K, HEADS)),

time: 52.3 us -> 53.3 us (1.019)
  Pallas kernels: 46.5 us -> 47.5 us
    pallas_call x1, Pallas kernels: 46.5 us -> 47.5 us  [on_device(): pl.pallas_call(functools.partial(kernel, rows, cols), out_shape=(jax.Shap...]
where the time goes in v2:
time: 53.3 us; the launch traced here: 53.1 us
  Pallas kernels  47.5 us (89%)
  local copies, waits for them, and re-layouts  5.02 us (9%)
  between operations  0.65 us (1%)
    pallas_call x1, Pallas kernels, on_device(): pl.pallas_call(functools.partial(kernel, rows, cols), out_shape=(jax.Shap...  47.5 us
    unnamed x10, local copies, waits for them, and re-layouts  5.02 us

profile of v2, /device:TPU:0, one launch (start us, length us, event | category | flops | bytes accessed | tf_op | source)
XLA Modules:
  0.0 53.1 jit_solution(13280232805159812615)
XLA Ops:
  0.6 0.0 copy-start
  0.6 0.9 %copy-done = bf16[128,512]{1,0:T(8,128)(2,1)S(1)} copy-done((bf16[128,512]{1,0:T(8,128)(2,1)S(1)}, bf16[128,512]{1,0:T(8,128)(2,1)}, u32[]{:S(2)}) %copy-start) | copy-done | bytes 131096
  1.5 0.0 copy-start.1
  1.5 0.9 %copy-done.1 = bf16[128,512]{1,0:T(8,128)(2,1)S(1)} copy-done((bf16[128,512]{1,0:T(8,128)(2,1)S(1)}, bf16[128,512]{1,0:T(8,128)(2,1)}, u32[]{:S(2)}) %copy-start.1) | copy-done | bytes 131096
  2.4 0.0 copy-start.2
  2.4 0.9 %copy-done.2 = bf16[128,512]{1,0:T(8,128)(2,1)S(1)} copy-done((bf16[128,512]{1,0:T(8,128)(2,1)S(1)}, bf16[128,512]{1,0:T(8,128)(2,1)}, u32[]{:S(2)}) %copy-start.2) | copy-done | bytes 131096
  3.3 0.0 copy-start.3
  3.3 0.9 %copy-done.3 = bf16[128,512]{1,0:T(8,128)(2,1)S(1)} copy-done((bf16[128,512]{1,0:T(8,128)(2,1)S(1)}, bf16[128,512]{1,0:T(8,128)(2,1)}, u32[]{:S(2)}) %copy-start.3) | copy-done | bytes 131096
  4.2 47.5 %shard_map.59 = (f32[128,512]{1,0:T(8,128)S(1)}, f32[128,512]{1,0:T(8,128)S(1)}) custom-call(bf16[128,512]{1,0:T(8,128)(2,1)S(1)} %copy-done, bf16[128,512]{1,0:T(8,128)(2,1)S(1)} %copy-done.1, bf16[128,512]{1,0:T(8,128)(2,1)S(1)} %copy-done.2, bf16[128,512]{1,0:T(8,128)(2,1)S(1)} %copy-done.3), custom_call_target="tpu_custom_call" | custom-call | flops 1610612736 | bytes 1572864 | tf_op jit(solution)/shard_map/pallas_call | solution.py:318
  51.7 0.7 %copy.8 = f32[128,512]{1,0:T(8,128)} copy(f32[128,512]{1,0:T(8,128)S(1)} %get-tuple-element.4) | data formatting | bytes 524288
  52.4 0.7 %copy.9 = f32[128,512]{1,0:T(8,128)} copy(f32[128,512]{1,0:T(8,128)S(1)} %get-tuple-element.5) | data formatting | bytes 524288
Async XLA Ops:
  0.6 0.9 %copy-start = (bf16[128,512]{1,0:T(8,128)(2,1)S(1)}, bf16[128,512]{1,0:T(8,128)(2,1)}, u32[]{:S(2)}) copy-start(bf16[128,512]{1,0:T(8,128)(2,1)} %rep_a.1) | copy-start | bytes 393220
  1.5 0.9 %copy-start.1 = (bf16[128,512]{1,0:T(8,128)(2,1)S(1)}, bf16[128,512]{1,0:T(8,128)(2,1)}, u32[]{:S(2)}) copy-start(bf16[128,512]{1,0:T(8,128)(2,1)} %val_a.1) | copy-start | bytes 393220
  2.4 0.9 %copy-start.2 = (bf16[128,512]{1,0:T(8,128)(2,1)S(1)}, bf16[128,512]{1,0:T(8,128)(2,1)}, u32[]{:S(2)}) copy-start(bf16[128,512]{1,0:T(8,128)(2,1)} %rep_b.1) | copy-start | bytes 393220
  3.3 0.9 %copy-start.3 = (bf16[128,512]{1,0:T(8,128)(2,1)S(1)}, bf16[128,512]{1,0:T(8,128)(2,1)}, u32[]{:S(2)}) copy-start(bf16[128,512]{1,0:T(8,128)(2,1)} %val_b.1) | copy-start | bytes 393220

commit v3 on v2

--- a/solution.py
+++ b/solution.py
@@ -11,14 +11,67 @@
 HEADS = 4
 HEAD = 128
 STATS = 8
+EXTRA = 16
+BINADES = 248.0
 MESH = pl.DeviceIdType.MESH
+
+
+def code_of(x, scale):
+    code = jnp.exp2(jnp.abs(x) * (BINADES / scale) - BINADES / 2)
+    return jnp.where(x < 0, -code, code).astype(jnp.bfloat16)
+
+
+def value_of(code, scale):
+    code = code.astype(jnp.float32)
+    size = jnp.log(jnp.abs(code)) * (1 / (math.log(2) * BINADES)) + 0.5
+    return jnp.where(code < 0, -size, size) * scale
+
+
+def scale_of(x):
+    largest = jnp.max(jnp.abs(x), axis=0, keepdims=True) * 1.01 + 1e-30
+    return largest.astype(jnp.bfloat16)
+
+
+def three_terms(x):
+    terms = []
+    for _ in range(3):
+        term = x.astype(jnp.bfloat16).astype(jnp.float32)
+        terms.append(term)
+        x = x - term
+    return terms
+
+
+def packed_part(num, total, peak):
+    mean = num / total
+    scale = scale_of(mean).astype(jnp.float32)
+    rows = [scale] + three_terms(peak) + three_terms(total)
+    sub = lax.broadcasted_iota(jnp.int32, (EXTRA, num.shape[1]), 0)
+    extra = jnp.zeros((EXTRA, num.shape[1]), jnp.float32)
+    for i, x in enumerate(rows):
+        extra = jnp.where(sub == i, x, extra)
+    return code_of(mean, scale), extra.astype(jnp.bfloat16)
+
+
+def unpacked_part(codes, extra):
+    extra = extra.astype(jnp.float32)
+    peak = extra[1:2] + extra[2:3] + extra[3:4]
+    total = extra[4:5] + extra[5:6] + extra[6:7]
+    return value_of(codes, extra[0:1]) * total, total, peak
+
+
+def merged(parts):
+    peak = functools.reduce(jnp.maximum, [x[2] for x in parts])
+    scales = [jnp.exp2(x[2] - peak) for x in parts]
+    num = sum(x[0] * w for x, w in zip(parts, scales))
+    total = sum(x[1] * w for x, w in zip(parts, scales))
+    return num, total, peak
 
 
 def kernel(
     rows, cols,
     rep_a, val_a, rep_b, val_b, out_a, out_b,
     in_a, in_b, keys_t, scores, peak_b,
-    part_a, got_a, part_b, mate_b, got_b, done_a, done_b,
+    part_a, code_a, got_a, part_b, mate_b, code_b, got_b, done_a, done_b, back_a, back_b,
     own, cut_a_send, cut_b_send, a_recv, b_recv, a_send, b_send, mate_send,
     part_a_send, got_a_recv, mate_b_send, mate_b_recv, part_b_send, got_b_recv,
     done_a_send, done_b_send, done_a_recv, done_b_recv,
@@ -156,14 +209,19 @@
         stats = jnp.where(lane == 0, peak, total)
         for kk in range(K):
             mine = slice(kk * n_a, (kk + 1) * n_a)
-            part_a[kk, pp, 0:HEAD] = num[mine].T
-            part_a[kk, pp, HEAD:HEAD + STATS] = stats[mine].T[0:STATS]
+            num_t = num[mine].T
+            stats_t = stats[mine].T[0:STATS]
+            part_a[kk, pp, 0:HEAD] = num_t
+            part_a[kk, pp, HEAD:HEAD + STATS] = stats_t
+            codes, extra = packed_part(num_t, stats_t[1:2], stats_t[0:1])
+            code_a[kk, pp, 0:HEAD] = codes
+            code_a[kk, pp, HEAD:HEAD + EXTRA] = extra
 
     def part_a_copy(d, e):
         there = (k + d) % K
         h = head_at(e)
         return remote(
-            part_a.at[there, h], got_a.at[k, h], part_a_send.at[d, e], got_a_recv.at[k, h], at_k(d)
+            code_a.at[there, h], got_a.at[k, h], part_a_send.at[d, e], got_a_recv.at[k, h], at_k(d)
         )
 
     def rows_of(e):
@@ -202,35 +260,38 @@
         )
 
     def part_b_copy(d, e):
-        there = (q + d) % Q * 2 + c
         h = head_at(e)
         return remote(
-            part_b.at[there, h], got_b.at[q, h], part_b_send.at[d, e], got_b_recv.at[q, h], at_q(d)
+            code_b.at[(q + d) % Q, h], got_b.at[q, h], part_b_send.at[d, e], got_b_recv.at[q, h], at_q(d)
         )
 
     order = [d % Q for d in range(1, Q + 1)]
 
-    def merged(parts):
-        peak = functools.reduce(jnp.maximum, [x[HEAD:HEAD + 1] for x in parts])
-        scales = [jnp.exp2(x[HEAD:HEAD + 1] - peak) for x in parts]
-        num = sum(x[0:HEAD] * w for x, w in zip(parts, scales))
-        total = sum(x[HEAD + 1:HEAD + 2] * w for x, w in zip(parts, scales))
-        return num, total, peak
-
-    def done_copy(e, done, out, send, recv):
-        return remote(done.at[head_at(e)], out.at[:, own_lanes], send.at[e], recv.at[p], at_head(e))
-
-    def wait_done(e, done, out, send, recv):
-        remote(
-            done.at[head_at(e)], out.at[:, head_lanes(head_at(e))], send.at[e], recv.at[head_at(e)], at_head(e)
-        ).wait_recv()
-
-    def finish(e, parts, done, out, send, recv):
+    def part_of(ref):
+        return ref[0:HEAD], ref[HEAD + 1:HEAD + 2], ref[HEAD:HEAD + 1]
+
+    def sent_part_of(ref):
+        return unpacked_part(ref[0:HEAD], ref[HEAD:HEAD + EXTRA])
+
+    def done_copy(e, done, back, send, recv):
+        return remote(done.at[head_at(e)], back.at[p], send.at[e], recv.at[p], at_head(e))
+
+    def take_done(e, done, back, out, send, recv):
+        h = head_at(e)
+        remote(done.at[h], back.at[h], send.at[e], recv.at[h], at_head(e)).wait_recv()
+        n = out.shape[0]
+        scale = back[h, n:n + EXTRA].astype(jnp.float32)[0:1]
+        out[:, head_lanes(h)] = value_of(back[h, 0:n], scale)
+
+    def finish(e, parts, done, back, out, send, recv):
         num, total, _ = merged(parts)
         result = (num / total).T
         if e:
-            done[head_at(e)] = result
-            done_copy(e, done, out, send, recv).start()
+            n = out.shape[0]
+            scale = scale_of(result)
+            done[head_at(e), 0:n] = code_of(result, scale.astype(jnp.float32))
+            done[head_at(e), n:n + EXTRA] = jnp.broadcast_to(scale, (EXTRA, HEAD))
+            done_copy(e, done, back, send, recv).start()
         else:
             out[:, own_lanes] = result
 
@@ -238,15 +299,15 @@
 
     def finish_a(e):
         h = head_at(e)
-        parts = [part_a[k, h]]
+        parts = [part_of(part_a.at[k, h])]
         for d in range(1, K):
             kk = (k + d) % K
             remote(
-                part_a.at[kk, h], got_a.at[kk, h], part_a_send.at[d, e], got_a_recv.at[kk, h],
+                code_a.at[kk, h], got_a.at[kk, h], part_a_send.at[d, e], got_a_recv.at[kk, h],
                 at_k(d),
             ).wait_recv()
-            parts.append(got_a[kk, h])
-        finish(e, parts, done_a, out_a, done_a_send, done_a_recv)
+            parts.append(sent_part_of(got_a.at[kk, h]))
+        finish(e, parts, done_a, back_a, out_a, done_a_send, done_a_recv)
 
     blocks = 2 * Q
     for i in range(blocks):
@@ -264,24 +325,33 @@
         mate_b_copy(d).wait_recv()
         for e in range(HEADS):
             h = head_at(e)
-            num, total, peak = merged([part_b[qq * 2 + c, h], mate_b[qq, h]])
-            part_b[qq * 2 + c, h, 0:HEAD] = num
-            part_b[qq * 2 + c, h, HEAD:HEAD + 1] = peak
-            part_b[qq * 2 + c, h, HEAD + 1:HEAD + 2] = total
+            both = merged([part_of(part_b.at[qq * 2 + c, h]), part_of(mate_b.at[qq, h])])
             if d:
+                codes, extra = packed_part(*both)
+                code_b[qq, h, 0:HEAD] = codes
+                code_b[qq, h, HEAD:HEAD + EXTRA] = extra
                 part_b_copy(d, e).start()
+            else:
+                part_b[qq * 2 + c, h, 0:HEAD] = both[0]
+                part_b[qq * 2 + c, h, HEAD:HEAD + 1] = both[2]
+                part_b[qq * 2 + c, h, HEAD + 1:HEAD + 2] = both[1]
 
     for e in last:
         h = head_at(e)
-        parts = [part_b[s, h]]
+        parts = [part_of(part_b.at[s, h])]
         for d in range(1, Q):
             qq = (q + d) % Q
             remote(
-                part_b.at[qq * 2 + c, h], got_b.at[qq, h], part_b_send.at[d, e],
+                code_b.at[qq, h], got_b.at[qq, h], part_b_send.at[d, e],
                 got_b_recv.at[qq, h], at_q(d),
             ).wait_recv()
-            parts.append(got_b[qq, h])
-        finish(e, parts, done_b, out_b, done_b_send, done_b_recv)
+            parts.append(sent_part_of(got_b.at[qq, h]))
+        finish(e, parts, done_b, back_b, out_b, done_b_send, done_b_recv)
+
+    for e in range(1, HEADS):
+        take_done(e, done_a, back_a, out_a, done_a_send, done_a_recv)
+    for e in range(1, HEADS):
+        take_done(e, done_b, back_b, out_b, done_b_send, done_b_recv)
 
     for d in range(1, HEADS):
         for i in range(2):
@@ -299,11 +369,8 @@
     for d in range(Q):
         mate_b_copy(d).wait_send()
     for e in range(1, HEADS):
-        done_copy(e, done_a, out_a, done_a_send, done_a_recv).wait_send()
-        done_copy(e, done_b, out_b, done_b_send, done_b_recv).wait_send()
-    for e in range(1, HEADS):
-        wait_done(e, done_a, out_a, done_a_send, done_a_recv)
-        wait_done(e, done_b, out_b, done_b_send, done_b_recv)
+        done_copy(e, done_a, back_a, done_a_send, done_a_recv).wait_send()
+        done_copy(e, done_b, back_b, done_b_send, done_b_recv).wait_send()
 
 
 def on_device(rows, cols, rep_a, val_a, rep_b, val_b):
@@ -330,12 +397,16 @@
             pltpu.VMEM((2 * Q, K * HEADS * n_a, HEADS * n_b), f32),
             pltpu.VMEM((2 * Q, 1, HEADS * n_b), f32),
             pltpu.VMEM((K, HEADS, tall, n_a), f32),
-            pltpu.VMEM((K, HEADS, tall, n_a), f32),
+            pltpu.VMEM((K, HEADS, HEAD + EXTRA, n_a), bf16),
+            pltpu.VMEM((K, HEADS, HEAD + EXTRA, n_a), bf16),
             pltpu.VMEM((2 * Q, HEADS, tall, n_b), f32),
             pltpu.VMEM((Q, HEADS, tall, n_b), f32),
-            pltpu.VMEM((Q, HEADS, tall, n_b), f32),
-            pltpu.VMEM((HEADS, n_a, HEAD), f32),
-            pltpu.VMEM((HEADS, n_b, HEAD), f32),
+            pltpu.VMEM((Q, HEADS, HEAD + EXTRA, n_b), bf16),
+            pltpu.VMEM((Q, HEADS, HEAD + EXTRA, n_b), bf16),
+            pltpu.VMEM((HEADS, n_a + EXTRA, HEAD), bf16),
+            pltpu.VMEM((HEADS, n_b + EXTRA, HEAD), bf16),
+            pltpu.VMEM((HEADS, n_a + EXTRA, HEAD), bf16),
+            pltpu.VMEM((HEADS, n_b + EXTRA, HEAD), bf16),
             dma((4,)), dma((HEADS, 2)), dma((HEADS, 2)),
             dma((K, HEADS)), dma((2 * Q, HEADS)),
             dma((K, HEADS)), dma((Q, HEADS)), dma((Q, HEADS)),
@@ -345,7 +416,7 @@
             dma((HEADS,)), dma((HEADS,)), dma((HEADS,)), dma((HEADS,)),
         ],
         compiler_params=pltpu.CompilerParams(
-            collective_id=0, has_side_effects=True, vmem_limit_bytes=48 * 1024 * 1024
+            collective_id=0, has_side_effects=True, vmem_limit_bytes=127 * 512 * 1024
         ),
         cost_estimate=pl.CostEstimate(
             flops=6 * tile * HEAD, bytes_accessed=6 * 1024 * (n_a + n_b), transcendentals=2 * tile

time: 53.3 us -> 48 us (0.901)
  Pallas kernels: 47.5 us -> 44.8 us
  local copies, waits for them, and re-layouts: 5.02 us -> 2.42 us
    pallas_call x1, Pallas kernels: 47.5 us -> 44.8 us  [on_device(): pl.pallas_call(functools.partial(kernel, rows, cols), out_shape=(jax.Shap...]
    unnamed x10 -> x4, local copies, waits for them, and re-layouts: 5.02 us -> 2.42 us
where the time goes in v3:
time: 48 us; the launch traced here: 47.9 us
  Pallas kernels  44.8 us (93%)
  local copies, waits for them, and re-layouts  2.42 us (5%)
  between operations  0.65 us (1%)
    pallas_call x1, Pallas kernels, on_device(): pl.pallas_call(functools.partial(kernel, rows, cols), out_shape=(jax.Shap...  44.8 us
    unnamed x4, local copies, waits for them, and re-layouts  2.42 us

profile of v3, /device:TPU:0, one launch (start us, length us, event | category | flops | bytes accessed | tf_op | source)
XLA Modules:
  0.0 47.9 jit_solution(14972696325830249339)
XLA Ops:
  0.6 44.8 %shard_map.59 = (f32[128,512]{1,0:T(8,128)}, f32[128,512]{1,0:T(8,128)}) custom-call(bf16[128,512]{1,0:T(8,128)(2,1)} %rep_a.1, bf16[128,512]{1,0:T(8,128)(2,1)} %val_a.1, bf16[128,512]{1,0:T(8,128)(2,1)} %rep_b.1, bf16[128,512]{1,0:T(8,128)(2,1)} %val_b.1), custom_call_target="tpu_custom_call" | custom-call | flops 1610612736 | bytes 1572864 | tf_op jit(solution)/shard_map/pallas_call | solution.py:385
  45.4 0.0 copy-start
  45.4 1.7 %copy.8 = f32[128,512]{1,0:T(8,128)} copy(f32[128,512]{1,0:T(8,128)} %get-tuple-element.4) | data formatting | bytes 524288
  47.2 0.0 copy-done
  47.2 0.7 %copy.9 = f32[128,512]{1,0:T(8,128)} copy(f32[128,512]{1,0:T(8,128)S(1)} %copy-done) | data formatting | bytes 524288
Async XLA Ops:
  45.4 1.7 %copy-start = (f32[128,512]{1,0:T(8,128)S(1)}, f32[128,512]{1,0:T(8,128)}, u32[]{:S(2)}) copy-start(f32[128,512]{1,0:T(8,128)} %get-tuple-element.5) | copy-start | bytes 786436

commit v4 on v3

--- a/solution.py
+++ b/solution.py
@@ -70,7 +70,7 @@
 def kernel(
     rows, cols,
     rep_a, val_a, rep_b, val_b, out_a, out_b,
-    in_a, in_b, keys_t, scores, peak_b,
+    in_a, in_b, keys_t, scores, peak_a, peak_b,
     part_a, code_a, got_a, part_b, mate_b, code_b, got_b, done_a, done_b, back_a, back_b,
     own, cut_a_send, cut_b_send, a_recv, b_recv, a_send, b_send, mate_send,
     part_a_send, got_a_recv, mate_b_send, mate_b_recv, part_b_send, got_b_recv,
@@ -129,82 +129,132 @@
     def cut_b_copy(d, i):
         return remote(
             (rep_b, val_b)[i].at[:, head_lanes(head_at(d))], in_b.at[s, p, i],
-            cut_b_send.at[d, i], b_recv.at[s, p], at_head(d),
+            cut_b_send.at[d, i], b_recv.at[s, p, i], at_head(d),
         )
 
     def cut_a_copy(d, i):
         return remote(
             (rep_a, val_a)[i].at[:, head_lanes(head_at(d))], in_a.at[p, k, i],
-            cut_a_send.at[d, i], a_recv.at[k, p], at_head(d),
-        )
-
-    def a_copy(d, e):
-        piece = in_a.at[head_at(e), k]
-        return remote(piece, piece, a_send.at[d, e], a_recv.at[k, head_at(e)], at_k(d))
-
-    def b_copy(d, e):
-        piece = in_b.at[s, head_at(e)]
-        return remote(piece, piece, b_send.at[d, e], b_recv.at[s, head_at(e)], at_q(d))
-
-    def mate_copy(d, e):
-        r = (q + d) % Q * 2 + c
-        piece = in_b.at[r, head_at(e)]
-        return remote(piece, piece, mate_send.at[d, e], b_recv.at[r, head_at(e)], mate)
-
-    def wait_b(r, e, device):
-        piece = in_b.at[r, head_at(e)]
-        remote(piece, piece, mate_send.at[0, 0], b_recv.at[r, head_at(e)], device).wait_recv()
-
-    def wait_a(r, e, device):
-        piece = in_a.at[head_at(e), r]
-        remote(piece, piece, mate_send.at[0, 0], a_recv.at[r, head_at(e)], device).wait_recv()
-
-    for cut in (cut_b_copy, cut_a_copy):
+            cut_a_send.at[d, i], a_recv.at[k, p, i], at_head(d),
+        )
+
+    def a_copy(d, e, i):
+        h = head_at(e)
+        piece = in_a.at[h, k, i]
+        return remote(piece, piece, a_send.at[d, e, i], a_recv.at[k, h, i], at_k(d))
+
+    def b_copy(d, e, i):
+        h = head_at(e)
+        piece = in_b.at[s, h, i]
+        return remote(piece, piece, b_send.at[d, e, i], b_recv.at[s, h, i], at_q(d))
+
+    def mate_copy(d, e, i):
+        r, h = (q + d) % Q * 2 + c, head_at(e)
+        piece = in_b.at[r, h, i]
+        return remote(piece, piece, mate_send.at[d, e, i], b_recv.at[r, h, i], mate)
+
+    def wait_b(r, e, i, device):
+        h = head_at(e)
+        piece = in_b.at[r, h, i]
+        remote(piece, piece, mate_send.at[0, 0, i], b_recv.at[r, h, i], device).wait_recv()
+
+    def wait_a(r, e, i, device):
+        h = head_at(e)
+        piece = in_a.at[h, r, i]
+        remote(piece, piece, mate_send.at[0, 0, i], a_recv.at[r, h, i], device).wait_recv()
+
+    def pass_b(e, i):
+        if e:
+            wait_b(s, e, i, at_head(e))
+        for d in range(1, Q):
+            b_copy(d, e, i).start()
+        mate_copy(0, e, i).start()
+
+    def pass_b_to_mate(e, i):
+        for d in range(1, Q):
+            wait_b((q + d) % Q * 2 + c, e, i, at_q(d))
+            mate_copy(d, e, i).start()
+
+    def end_b(e, i):
+        for d in range(Q):
+            wait_b((q + d) % Q * 2 + 1 - c, e, i, mate)
+
+    def pass_a(e, i):
+        if e:
+            wait_a(k, e, i, at_head(e))
+        for d in range(1, K):
+            a_copy(d, e, i).start()
+
+    def end_a(e, i):
+        for d in range(1, K):
+            wait_a((k + d) % K, e, i, at_k(d))
+
+    heads = range(HEADS)
+    for cut, i in ((cut_b_copy, 0), (cut_a_copy, 0), (cut_a_copy, 1), (cut_b_copy, 1)):
         for d in range(1, HEADS):
-            for i in range(2):
-                cut(d, i).start()
+            cut(d, i).start()
     for copy in own_copies:
         copy.wait()
-    for e in range(HEADS):
-        if e:
-            wait_b(s, e, at_head(e))
-        for d in range(1, Q):
-            b_copy(d, e).start()
-        mate_copy(0, e).start()
-        if e == 0:
-            for d in range(1, K):
-                a_copy(d, 0).start()
-    for e in range(HEADS):
-        for d in range(1, Q):
-            wait_b((q + d) % Q * 2 + c, e, at_q(d))
-            mate_copy(d, e).start()
-    for e in range(HEADS):
-        for d in range(Q):
-            wait_b((q + d) % Q * 2 + 1 - c, e, mate)
-    for r in range(2 * Q):
-        keys_t[r] = in_b[r, :, 0].reshape(HEADS * n_b, HEAD).T
+    pass_b(0, 0)
+    pass_a(0, 0)
+    pass_a(0, 1)
+    for e in range(1, HEADS):
+        pass_b(e, 0)
+        pass_b_to_mate(e - 1, 0)
+    pass_b(0, 1)
+    pass_a(1, 0)
+    pass_b_to_mate(HEADS - 1, 0)
 
     width = HEADS * n_b
     span = K * n_a
-
-    def row_block(pp):
-        start = pl.multiple_of(pp * span, span)
-        queries = in_a[pp, :, 0].reshape(span, HEAD)
-        peak = jnp.full((span, 1), -jnp.inf, jnp.float32)
+    for d in range(Q):
+        r = (q + d) % Q * 2 + c
+        keys_t[r] = in_b[r, :, 0].reshape(width, HEAD).T
+    for e in heads:
+        end_b(e, 0)
+    for d in range(Q):
+        r = (q + d) % Q * 2 + 1 - c
+        keys_t[r] = in_b[r, :, 0].reshape(width, HEAD).T
+
+    def rows_at(e):
+        return pl.ds(pl.multiple_of(head_at(e) * span, span), span)
+
+    def lane_groups(x):
+        return [x[:, j:j + HEAD] for j in range(0, width, HEAD)]
+
+    def score_block(e):
+        queries = in_a[head_at(e), :, 0].reshape(span, HEAD)
+        peak = jnp.full((span, HEAD), -jnp.inf, jnp.float32)
         for r in range(2 * Q):
             logits = jnp.dot(queries, keys_t[r], preferred_element_type=jnp.float32) * to_log2
-            scores[r, pl.ds(start, span), :] = logits
-            peak_b[r] = jnp.maximum(peak_b[r], jnp.max(logits, axis=0, keepdims=True))
-            peak = jnp.maximum(peak, jnp.max(logits, axis=1, keepdims=True))
-        total = jnp.zeros((span, 1), jnp.float32)
+            scores[r, rows_at(e), :] = logits
+            tops = jnp.max(logits.reshape(span // 8, 8, width), axis=0)
+            peak_b[r] = jnp.maximum(peak_b[r], tops)
+            peak = functools.reduce(jnp.maximum, lane_groups(logits), peak)
+        peak_a[e] = peak
+
+    for e in heads:
+        if e + 1 < HEADS:
+            if e:
+                pass_a(e + 1, 0)
+        end_a(e, 0)
+        score_block(e)
+        if e:
+            pass_a(e, 1)
+
+    def row_block(e):
+        pp = head_at(e)
+        peak = jnp.max(peak_a[e], axis=1, keepdims=True)
+        totals = jnp.zeros((span, HEAD), jnp.float32)
         num = jnp.zeros((span, HEAD), jnp.float32)
         for r in range(2 * Q):
             values = in_b[r, :, 1].reshape(width, HEAD)
-            weights = jnp.exp2(scores[r, pl.ds(start, span), :] - peak)
-            total += jnp.sum(weights, axis=1, keepdims=True)
+            weights = jnp.exp2(scores[r, rows_at(e), :] - peak)
+            totals = functools.reduce(jnp.add, lane_groups(weights), totals)
             num += jnp.dot(
                 weights.astype(jnp.bfloat16), values, preferred_element_type=jnp.float32
             )
+        total = jnp.sum(totals, axis=1, keepdims=True)
         lane = lax.broadcasted_iota(jnp.int32, (span, HEAD), 1)
         stats = jnp.where(lane == 0, peak, total)
         for kk in range(K):
@@ -224,26 +274,12 @@
             code_a.at[there, h], got_a.at[k, h], part_a_send.at[d, e], got_a_recv.at[k, h], at_k(d)
         )
 
-    def rows_of(e):
-        for d in range(1, K):
-            wait_a((k + d) % K, e, at_k(d))
-        row_block(head_at(e))
-        for d in range(1, K):
-            part_a_copy(d, e).start()
-
-    @pl.loop(0, HEADS - 1)
-    def _(e):
-        wait_a(k, e + 1, at_head(e + 1))
-        for d in range(1, K):
-            a_copy(d, e + 1).start()
-        rows_of(e)
-
-    rows_of(HEADS - 1)
-
+    for e in heads:
+        end_a(e, 1)
     values_t = in_a[:, :, 1].reshape(HEADS * span, HEAD).T
 
     def col_block(r):
-        peak = peak_b[r]
+        peak = jnp.max(peak_b[r], axis=0, keepdims=True)
         weights = jnp.exp2(scores[r] - peak)
         total = jnp.sum(weights, axis=0, keepdims=True)
         num = jnp.dot(values_t, weights.astype(jnp.bfloat16), preferred_element_type=jnp.float32)
@@ -309,18 +345,19 @@
             parts.append(sent_part_of(got_a.at[kk, h]))
         finish(e, parts, done_a, back_a, out_a, done_a_send, done_a_recv)
 
-    blocks = 2 * Q
-    for i in range(blocks):
-        d = order[i % Q]
-        if i < Q:
-            col_block((q + d) % Q * 2 + 1 - c)
-            mate_b_copy(d).start()
-        else:
-            col_block((q + d) % Q * 2 + c)
-        for e in last[i * HEADS // blocks:(i + 1) * HEADS // blocks]:
-            finish_a(e)
-
-    for d in order:
+    def finish_b(e):
+        h = head_at(e)
+        parts = [part_of(part_b.at[s, h])]
+        for d in range(1, Q):
+            qq = (q + d) % Q
+            remote(
+                code_b.at[qq, h], got_b.at[qq, h], part_b_send.at[d, e],
+                got_b_recv.at[qq, h], at_q(d),
+            ).wait_recv()
+            parts.append(sent_part_of(got_b.at[qq, h]))
+        finish(e, parts, done_b, back_b, out_b, done_b_send, done_b_recv)
+
+    def merge_mate(d):
         qq = (q + d) % Q
         mate_b_copy(d).wait_recv()
         for e in range(HEADS):
@@ -336,22 +373,32 @@
                 part_b[qq * 2 + c, h, HEAD:HEAD + 1] = both[2]
                 part_b[qq * 2 + c, h, HEAD + 1:HEAD + 2] = both[1]
 
-    for e in last:
-        h = head_at(e)
-        parts = [part_of(part_b.at[s, h])]
-        for d in range(1, Q):
-            qq = (q + d) % Q
-            remote(
-                code_b.at[qq, h], got_b.at[qq, h], part_b_send.at[d, e],
-                got_b_recv.at[qq, h], at_q(d),
-            ).wait_recv()
-            parts.append(sent_part_of(got_b.at[qq, h]))
-        finish(e, parts, done_b, back_b, out_b, done_b_send, done_b_recv)
-
+    for n, d in enumerate(order):
+        col_block((q + d) % Q * 2 + 1 - c)
+        mate_b_copy(d).start()
+        if n == 0:
+            for e in range(1, HEADS):
+                pass_b(e, 1)
+    for e in heads:
+        pass_b_to_mate(e, 1)
+    for d in order:
+        col_block((q + d) % Q * 2 + c)
+        merge_mate(d)
+    for e in heads:
+        end_b(e, 1)
+
+    for n, e in enumerate(last):
+        row_block(e)
+        for d in range(1, K):
+            part_a_copy(d, e).start()
+        if n:
+            finish_a(last[n - 1])
+        finish_b(e)
+    finish_a(last[-1])
+    for e in range(1, HEADS):
+        take_done(e, done_b, back_b, out_b, done_b_send, done_b_recv)
     for e in range(1, HEADS):
         take_done(e, done_a, back_a, out_a, done_a_send, done_a_recv)
-    for e in range(1, HEADS):
-        take_done(e, done_b, back_b, out_b, done_b_send, done_b_recv)
 
     for d in range(1, HEADS):
         for i in range(2):
@@ -359,13 +406,16 @@
             cut_a_copy(d, i).wait_send()
     for e in range(HEADS):
         for d in range(1, K):
-            a_copy(d, e).wait_send()
+            for i in range(2):
+                a_copy(d, e, i).wait_send()
             part_a_copy(d, e).wait_send()
         for d in range(Q):
             if d:
-                b_copy(d, e).wait_send()
+                for i in range(2):
+                    b_copy(d, e, i).wait_send()
                 part_b_copy(d, e).wait_send()
-            mate_copy(d, e).wait_send()
+            for i in range(2):
+                mate_copy(d, e, i).wait_send()
     for d in range(Q):
         mate_b_copy(d).wait_send()
     for e in range(1, HEADS):
@@ -395,7 +445,8 @@
             pltpu.VMEM((2 * Q, HEADS, 2, n_b, HEAD), bf16),
             pltpu.VMEM((2 * Q, HEAD, HEADS * n_b), bf16),
             pltpu.VMEM((2 * Q, K * HEADS * n_a, HEADS * n_b), f32),
-            pltpu.VMEM((2 * Q, 1, HEADS * n_b), f32),
+            pltpu.VMEM((HEADS, K * n_a, HEAD), f32),
+            pltpu.VMEM((2 * Q, 8, HEADS * n_b), f32),
             pltpu.VMEM((K, HEADS, tall, n_a), f32),
             pltpu.VMEM((K, HEADS, HEAD + EXTRA, n_a), bf16),
             pltpu.VMEM((K, HEADS, HEAD + EXTRA, n_a), bf16),
@@ -408,8 +459,8 @@
             pltpu.VMEM((HEADS, n_a + EXTRA, HEAD), bf16),
             pltpu.VMEM((HEADS, n_b + EXTRA, HEAD), bf16),
             dma((4,)), dma((HEADS, 2)), dma((HEADS, 2)),
-            dma((K, HEADS)), dma((2 * Q, HEADS)),
-            dma((K, HEADS)), dma((Q, HEADS)), dma((Q, HEADS)),
+            dma((K, HEADS, 2)), dma((2 * Q, HEADS, 2)),
+            dma((K, HEADS, 2)), dma((Q, HEADS, 2)), dma((Q, HEADS, 2)),
             dma((K, HEADS)), dma((K, HEADS)),
             dma((Q,)), dma((Q,)),
             dma((Q, HEADS)), dma((Q, HEADS)),

time: 48 us -> 48.9 us (1.019)
  Pallas kernels: 44.8 us -> 45.7 us
    pallas_call x1, Pallas kernels: 44.8 us -> 45.7 us  [on_device(): pl.pallas_call(functools.partial(kernel, rows, cols), out_shape=(jax.Shap...]
where the time goes in v4:
time: 48.9 us; the launch traced here: 48.7 us
  Pallas kernels  45.7 us (93%)
  local copies, waits for them, and re-layouts  2.42 us (5%)
  between operations  0.65 us (1%)
    pallas_call x1, Pallas kernels, on_device(): pl.pallas_call(functools.partial(kernel, rows, cols), out_shape=(jax.Shap...  45.7 us
    unnamed x4, local copies, waits for them, and re-layouts  2.42 us

profile of v4, /device:TPU:0, one launch (start us, length us, event | category | flops | bytes accessed | tf_op | source)
XLA Modules:
  0.0 48.7 jit_solution(5596768150008134990)
XLA Ops:
  0.6 45.7 %shard_map.59 = (f32[128,512]{1,0:T(8,128)}, f32[128,512]{1,0:T(8,128)}) custom-call(bf16[128,512]{1,0:T(8,128)(2,1)} %rep_a.1, bf16[128,512]{1,0:T(8,128)(2,1)} %val_a.1, bf16[128,512]{1,0:T(8,128)(2,1)} %rep_b.1, bf16[128,512]{1,0:T(8,128)(2,1)} %val_b.1), custom_call_target="tpu_custom_call" | custom-call | flops 1610612736 | bytes 1572864 | tf_op jit(solution)/shard_map/pallas_call | solution.py:435
  46.3 0.0 copy-start
  46.3 1.7 %copy.8 = f32[128,512]{1,0:T(8,128)} copy(f32[128,512]{1,0:T(8,128)} %get-tuple-element.4) | data formatting | bytes 524288
  48.0 0.0 copy-done
  48.0 0.7 %copy.9 = f32[128,512]{1,0:T(8,128)} copy(f32[128,512]{1,0:T(8,128)S(1)} %copy-done) | data formatting | bytes 524288
Async XLA Ops:
  46.3 1.7 %copy-start = (f32[128,512]{1,0:T(8,128)S(1)}, f32[128,512]{1,0:T(8,128)}, u32[]{:S(2)}) copy-start(f32[128,512]{1,0:T(8,128)} %get-tuple-element.5) | copy-start | bytes 786436

commit v5 on v4

--- a/solution.py
+++ b/solution.py
@@ -70,7 +70,7 @@
 def kernel(
     rows, cols,
     rep_a, val_a, rep_b, val_b, out_a, out_b,
-    in_a, in_b, keys_t, scores, peak_a, peak_b,
+    in_a, in_b, keys_t, values_t, scores, peak_a, peak_b,
     part_a, code_a, got_a, part_b, mate_b, code_b, got_b, done_a, done_b, back_a, back_b,
     own, cut_a_send, cut_b_send, a_recv, b_recv, a_send, b_send, mate_send,
     part_a_send, got_a_recv, mate_b_send, mate_b_recv, part_b_send, got_b_recv,
@@ -79,22 +79,22 @@
     Q, K = rows // HEADS, cols // 2
     n_a, n_b = rep_a.shape[0], rep_b.shape[0]
     row, col = lax.axis_index("row"), lax.axis_index("col")
-    p, q = row // Q, row % Q
-    k, c = col // 2, col % 2
+    p, q = lax.div(row, Q), lax.rem(row, Q)
+    k, c = lax.div(col, 2), lax.rem(col, 2)
     s = q * 2 + c
     to_log2 = HEAD ** -0.5 * math.log2(math.e)
 
     def head_at(d):
-        return (p + d) % HEADS
+        return lax.rem(p + d, HEADS)
 
     def at_head(d):
         return (head_at(d) * Q + q, col)
 
     def at_k(d):
-        return (row, (k + d) % K * 2 + c)
+        return (row, lax.rem(k + d, K) * 2 + c)
 
     def at_q(d):
-        return (p * Q + (q + d) % Q, col)
+        return (p * Q + lax.rem(q + d, Q), col)
 
     mate = (row, k * 2 + 1 - c)
 
@@ -149,7 +149,7 @@
         return remote(piece, piece, b_send.at[d, e, i], b_recv.at[s, h, i], at_q(d))
 
     def mate_copy(d, e, i):
-        r, h = (q + d) % Q * 2 + c, head_at(e)
+        r, h = lax.rem(q + d, Q) * 2 + c, head_at(e)
         piece = in_b.at[r, h, i]
         return remote(piece, piece, mate_send.at[d, e, i], b_recv.at[r, h, i], mate)
 
@@ -163,8 +163,8 @@
         piece = in_a.at[h, r, i]
         remote(piece, piece, mate_send.at[0, 0, i], a_recv.at[r, h, i], device).wait_recv()
 
-    def pass_b(e, i):
-        if e:
+    def pass_b(e, i, own=False):
+        if not own:
             wait_b(s, e, i, at_head(e))
         for d in range(1, Q):
             b_copy(d, e, i).start()
@@ -172,48 +172,45 @@
 
     def pass_b_to_mate(e, i):
         for d in range(1, Q):
-            wait_b((q + d) % Q * 2 + c, e, i, at_q(d))
+            wait_b(lax.rem(q + d, Q) * 2 + c, e, i, at_q(d))
             mate_copy(d, e, i).start()
 
     def end_b(e, i):
         for d in range(Q):
-            wait_b((q + d) % Q * 2 + 1 - c, e, i, mate)
-
-    def pass_a(e, i):
-        if e:
+            wait_b(lax.rem(q + d, Q) * 2 + 1 - c, e, i, mate)
+
+    def pass_a(e, i, own=False):
+        if not own:
             wait_a(k, e, i, at_head(e))
         for d in range(1, K):
             a_copy(d, e, i).start()
 
     def end_a(e, i):
         for d in range(1, K):
-            wait_a((k + d) % K, e, i, at_k(d))
-
-    heads = range(HEADS)
+            wait_a(lax.rem(k + d, K), e, i, at_k(d))
+
     for cut, i in ((cut_b_copy, 0), (cut_a_copy, 0), (cut_a_copy, 1), (cut_b_copy, 1)):
-        for d in range(1, HEADS):
-            cut(d, i).start()
+        pl.loop(1, HEADS)(lambda d, cut=cut, i=i: cut(d, i).start())
     for copy in own_copies:
         copy.wait()
-    pass_b(0, 0)
-    pass_a(0, 0)
-    pass_a(0, 1)
-    for e in range(1, HEADS):
+    for i in range(2):
+        pass_b(0, i, own=True)
+        pass_a(0, i, own=True)
+
+    @pl.loop(1, HEADS)
+    def _(e):
         pass_b(e, 0)
         pass_b_to_mate(e - 1, 0)
-    pass_b(0, 1)
-    pass_a(1, 0)
+
     pass_b_to_mate(HEADS - 1, 0)
+    pl.loop(1, HEADS)(lambda e: pass_a(e, 0))
 
     width = HEADS * n_b
     span = K * n_a
-    for d in range(Q):
-        r = (q + d) % Q * 2 + c
-        keys_t[r] = in_b[r, :, 0].reshape(width, HEAD).T
-    for e in heads:
-        end_b(e, 0)
-    for d in range(Q):
-        r = (q + d) % Q * 2 + 1 - c
+    pl.loop(0, HEADS)(lambda e: end_b(e, 0))
+
+    @pl.loop(0, 2 * Q)
+    def _(r):
         keys_t[r] = in_b[r, :, 0].reshape(width, HEAD).T
 
     def rows_at(e):
@@ -233,13 +230,13 @@
             peak = functools.reduce(jnp.maximum, lane_groups(logits), peak)
         peak_a[e] = peak
 
-    for e in heads:
-        if e + 1 < HEADS:
-            if e:
-                pass_a(e + 1, 0)
+    @pl.loop(0, HEADS)
+    def _(e):
         end_a(e, 0)
         score_block(e)
-        if e:
+
+        @pl.when(e > 0)
+        def _():
             pass_a(e, 1)
 
     def row_block(e):
@@ -268,21 +265,20 @@
             code_a[kk, pp, HEAD:HEAD + EXTRA] = extra
 
     def part_a_copy(d, e):
-        there = (k + d) % K
+        there = lax.rem(k + d, K)
         h = head_at(e)
         return remote(
             code_a.at[there, h], got_a.at[k, h], part_a_send.at[d, e], got_a_recv.at[k, h], at_k(d)
         )
 
-    for e in heads:
-        end_a(e, 1)
-    values_t = in_a[:, :, 1].reshape(HEADS * span, HEAD).T
+    pl.loop(0, HEADS)(lambda e: end_a(e, 1))
+    values_t[...] = in_a[:, :, 1].reshape(HEADS * span, HEAD).T
 
     def col_block(r):
         peak = jnp.max(peak_b[r], axis=0, keepdims=True)
         weights = jnp.exp2(scores[r] - peak)
         total = jnp.sum(weights, axis=0, keepdims=True)
-        num = jnp.dot(values_t, weights.astype(jnp.bfloat16), preferred_element_type=jnp.float32)
+        num = jnp.dot(values_t[...], weights.astype(jnp.bfloat16), preferred_element_type=jnp.float32)
         sub = lax.broadcasted_iota(jnp.int32, (STATS, width), 0)
         stats = jnp.where(sub == 0, peak, total)
         for h in range(HEADS):
@@ -290,7 +286,7 @@
             part_b[r, h, HEAD:HEAD + STATS] = stats[:, h * n_b:(h + 1) * n_b]
 
     def mate_b_copy(d):
-        qq = (q + d) % Q
+        qq = lax.rem(q + d, Q)
         return remote(
             part_b.at[qq * 2 + 1 - c], mate_b.at[qq], mate_b_send.at[d], mate_b_recv.at[qq], mate
         )
@@ -298,10 +294,8 @@
     def part_b_copy(d, e):
         h = head_at(e)
         return remote(
-            code_b.at[(q + d) % Q, h], got_b.at[q, h], part_b_send.at[d, e], got_b_recv.at[q, h], at_q(d)
+            code_b.at[lax.rem(q + d, Q), h], got_b.at[q, h], part_b_send.at[d, e], got_b_recv.at[q, h], at_q(d)
         )
-
-    order = [d % Q for d in range(1, Q + 1)]
 
     def part_of(ref):
         return ref[0:HEAD], ref[HEAD + 1:HEAD + 2], ref[HEAD:HEAD + 1]
@@ -322,22 +316,24 @@
     def finish(e, parts, done, back, out, send, recv):
         num, total, _ = merged(parts)
         result = (num / total).T
-        if e:
+
+        @pl.when(e > 0)
+        def _():
             n = out.shape[0]
             scale = scale_of(result)
             done[head_at(e), 0:n] = code_of(result, scale.astype(jnp.float32))
             done[head_at(e), n:n + EXTRA] = jnp.broadcast_to(scale, (EXTRA, HEAD))
             done_copy(e, done, back, send, recv).start()
-        else:
+
+        @pl.when(e == 0)
+        def _():
             out[:, own_lanes] = result
-
-    last = [d % HEADS for d in range(1, HEADS + 1)]
 
     def finish_a(e):
         h = head_at(e)
         parts = [part_of(part_a.at[k, h])]
         for d in range(1, K):
-            kk = (k + d) % K
+            kk = lax.rem(k + d, K)
             remote(
                 code_a.at[kk, h], got_a.at[kk, h], part_a_send.at[d, e], got_a_recv.at[kk, h],
                 at_k(d),
@@ -349,7 +345,7 @@
         h = head_at(e)
         parts = [part_of(part_b.at[s, h])]
         for d in range(1, Q):
-            qq = (q + d) % Q
+            qq = lax.rem(q + d, Q)
             remote(
                 code_b.at[qq, h], got_b.at[qq, h], part_b_send.at[d, e],
                 got_b_recv.at[qq, h], at_q(d),
@@ -358,69 +354,96 @@
         finish(e, parts, done_b, back_b, out_b, done_b_send, done_b_recv)
 
     def merge_mate(d):
-        qq = (q + d) % Q
+        qq = lax.rem(q + d, Q)
         mate_b_copy(d).wait_recv()
-        for e in range(HEADS):
+
+        @pl.loop(0, HEADS)
+        def _(e):
             h = head_at(e)
             both = merged([part_of(part_b.at[qq * 2 + c, h]), part_of(mate_b.at[qq, h])])
-            if d:
+
+            @pl.when(d > 0)
+            def _():
                 codes, extra = packed_part(*both)
                 code_b[qq, h, 0:HEAD] = codes
                 code_b[qq, h, HEAD:HEAD + EXTRA] = extra
                 part_b_copy(d, e).start()
-            else:
+
+            @pl.when(d == 0)
+            def _():
                 part_b[qq * 2 + c, h, 0:HEAD] = both[0]
                 part_b[qq * 2 + c, h, HEAD:HEAD + 1] = both[2]
                 part_b[qq * 2 + c, h, HEAD + 1:HEAD + 2] = both[1]
 
-    for n, d in enumerate(order):
-        col_block((q + d) % Q * 2 + 1 - c)
-        mate_b_copy(d).start()
-        if n == 0:
-            for e in range(1, HEADS):
-                pass_b(e, 1)
-    for e in heads:
-        pass_b_to_mate(e, 1)
-    for d in order:
-        col_block((q + d) % Q * 2 + c)
-        merge_mate(d)
-    for e in heads:
-        end_b(e, 1)
-
-    for n, e in enumerate(last):
-        row_block(e)
-        for d in range(1, K):
-            part_a_copy(d, e).start()
-        if n:
-            finish_a(last[n - 1])
-        finish_b(e)
-    finish_a(last[-1])
-    for e in range(1, HEADS):
+    @pl.loop(0, 2 * Q)
+    def _(t):
+        d = lax.rem(t + 1, Q)
+        first = t < Q
+        col_block(lax.rem(q + d, Q) * 2 + jnp.where(first, 1 - c, c))
+
+        @pl.when(first)
+        def _():
+            mate_b_copy(d).start()
+
+        @pl.when(t == 0)
+        def _():
+            pl.loop(1, HEADS)(lambda e: pass_b(e, 1))
+
+        @pl.when(t == Q - 1)
+        def _():
+            pl.loop(0, HEADS)(lambda e: pass_b_to_mate(e, 1))
+
+        @pl.when(t >= Q)
+        def _():
+            merge_mate(d)
+
+    pl.loop(0, HEADS)(lambda e: end_b(e, 1))
+
+    @pl.loop(0, HEADS + 1)
+    def _(n):
+        @pl.when(n < HEADS)
+        def _():
+            e = lax.rem(n + 1, HEADS)
+            row_block(e)
+            for d in range(1, K):
+                part_a_copy(d, e).start()
+            finish_b(e)
+
+        @pl.when(n > 0)
+        def _():
+            finish_a(lax.rem(n, HEADS))
+
+    @pl.loop(1, HEADS)
+    def _(e):
         take_done(e, done_b, back_b, out_b, done_b_send, done_b_recv)
-    for e in range(1, HEADS):
+
+    @pl.loop(1, HEADS)
+    def _(e):
         take_done(e, done_a, back_a, out_a, done_a_send, done_a_recv)
 
-    for d in range(1, HEADS):
+    @pl.loop(1, HEADS)
+    def _(e):
         for i in range(2):
-            cut_b_copy(d, i).wait_send()
-            cut_a_copy(d, i).wait_send()
-    for e in range(HEADS):
+            cut_b_copy(e, i).wait_send()
+            cut_a_copy(e, i).wait_send()
+        done_copy(e, done_a, back_a, done_a_send, done_a_recv).wait_send()
+        done_copy(e, done_b, back_b, done_b_send, done_b_recv).wait_send()
+
+    @pl.loop(0, HEADS)
+    def _(e):
         for d in range(1, K):
             for i in range(2):
                 a_copy(d, e, i).wait_send()
             part_a_copy(d, e).wait_send()
         for d in range(Q):
+            for i in range(2):
+                if d:
+                    b_copy(d, e, i).wait_send()
+                mate_copy(d, e, i).wait_send()
             if d:
-                for i in range(2):
-                    b_copy(d, e, i).wait_send()
                 part_b_copy(d, e).wait_send()
-            for i in range(2):
-                mate_copy(d, e, i).wait_send()
-    for d in range(Q):
-        mate_b_copy(d).wait_send()
-    for e in range(1, HEADS):
-        done_copy(e, done_a, back_a, done_a_send, done_a_recv).wait_send()
-        done_copy(e, done_b, back_b, done_b_send, done_b_recv).wait_send()
+
+    pl.loop(0, Q)(lambda d: mate_b_copy(d).wait_send())
 
 
 def on_device(rows, cols, rep_a, val_a, rep_b, val_b):
@@ -444,6 +467,7 @@
             pltpu.VMEM((HEADS, K, 2, n_a, HEAD), bf16),
             pltpu.VMEM((2 * Q, HEADS, 2, n_b, HEAD), bf16),
             pltpu.VMEM((2 * Q, HEAD, HEADS * n_b), bf16),
+            pltpu.VMEM((HEAD, HEADS * K * n_a), bf16),
             pltpu.VMEM((2 * Q, K * HEADS * n_a, HEADS * n_b), f32),
             pltpu.VMEM((HEADS, K * n_a, HEAD), f32),
             pltpu.VMEM((2 * Q, 8, HEADS * n_b), f32),

time: 48.9 us -> 48 us (0.982)
  Pallas kernels: 45.7 us -> 44.7 us
    pallas_call x1, Pallas kernels: 45.7 us -> 44.7 us  [on_device(): pl.pallas_call(functools.partial(kernel, rows, cols), out_shape=(jax.Shap...]
where the time goes in v5:
time: 48 us; the launch traced here: 47.8 us
  Pallas kernels  44.7 us (93%)
  local copies, waits for them, and re-layouts  2.42 us (5%)
  between operations  0.65 us (1%)
    pallas_call x1, Pallas kernels, on_device(): pl.pallas_call(functools.partial(kernel, rows, cols), out_shape=(jax.Shap...  44.7 us
    unnamed x4, local copies, waits for them, and re-layouts  2.42 us

profile of v5, /device:TPU:0, one launch (start us, length us, event | category | flops | bytes accessed | tf_op | source)
XLA Modules:
  0.0 47.8 jit_solution(798148408478734565)
XLA Ops:
  0.6 44.7 %shard_map.59 = (f32[128,512]{1,0:T(8,128)}, f32[128,512]{1,0:T(8,128)}) custom-call(bf16[128,512]{1,0:T(8,128)(2,1)} %rep_a.1, bf16[128,512]{1,0:T(8,128)(2,1)} %val_a.1, bf16[128,512]{1,0:T(8,128)(2,1)} %rep_b.1, bf16[128,512]{1,0:T(8,128)(2,1)} %val_b.1), custom_call_target="tpu_custom_call" | custom-call | flops 1610612736 | bytes 1572864 | tf_op jit(solution)/shard_map/pallas_call | solution.py:458
  45.4 0.0 copy-start
  45.4 1.7 %copy.8 = f32[128,512]{1,0:T(8,128)} copy(f32[128,512]{1,0:T(8,128)} %get-tuple-element.4) | data formatting | bytes 524288
  47.1 0.0 copy-done
  47.1 0.7 %copy.9 = f32[128,512]{1,0:T(8,128)} copy(f32[128,512]{1,0:T(8,128)S(1)} %copy-done) | data formatting | bytes 524288
Async XLA Ops:
  45.4 1.7 %copy-start = (f32[128,512]{1,0:T(8,128)S(1)}, f32[128,512]{1,0:T(8,128)}, u32[]{:S(2)}) copy-start(f32[128,512]{1,0:T(8,128)} %get-tuple-element.5) | copy-start | bytes 786436

commit v6 on v5

--- a/solution.py
+++ b/solution.py
@@ -13,6 +13,7 @@
 STATS = 8
 EXTRA = 16
 BINADES = 248.0
+GRANT = 127 * 512 * 1024
 MESH = pl.DeviceIdType.MESH
 
 
@@ -69,9 +70,9 @@
 
 def kernel(
     rows, cols,
-    rep_a, val_a, rep_b, val_b, out_a, out_b,
-    in_a, in_b, keys_t, values_t, scores, peak_a, peak_b,
-    part_a, code_a, got_a, part_b, mate_b, code_b, got_b, done_a, done_b, back_a, back_b,
+    rep_a, val_a, rep_b, val_b, back_a, back_b,
+    in_a, in_b, values_t, scores, peak_a, peak_b,
+    part_a, code_a, got_a, part_b, mate_b, code_b, got_b, done_a, done_b,
     own, cut_a_send, cut_b_send, a_recv, b_recv, a_send, b_send, mate_send,
     part_a_send, got_a_recv, mate_b_send, mate_b_recv, part_b_send, got_b_recv,
     done_a_send, done_b_send, done_a_recv, done_b_recv,
@@ -123,7 +124,7 @@
     ]
     for copy in own_copies:
         copy.start()
-    peak_b[...] = jnp.full_like(peak_b, -jnp.inf)
+    peak_a[...] = jnp.full_like(peak_a, -jnp.inf)
     pl.semaphore_wait(barrier, len(peers))
 
     def cut_b_copy(d, i):
@@ -189,59 +190,66 @@
         for d in range(1, K):
             wait_a(lax.rem(k + d, K), e, i, at_k(d))
 
-    for cut, i in ((cut_b_copy, 0), (cut_a_copy, 0), (cut_a_copy, 1), (cut_b_copy, 1)):
+    for cut, i in ((cut_a_copy, 0), (cut_b_copy, 0), (cut_a_copy, 1), (cut_b_copy, 1)):
         pl.loop(1, HEADS)(lambda d, cut=cut, i=i: cut(d, i).start())
     for copy in own_copies:
         copy.wait()
     for i in range(2):
+        pass_a(0, i, own=True)
         pass_b(0, i, own=True)
-        pass_a(0, i, own=True)
+    pl.loop(1, HEADS)(lambda e: pass_a(e, 0))
 
     @pl.loop(1, HEADS)
     def _(e):
         pass_b(e, 0)
         pass_b_to_mate(e - 1, 0)
 
-    pass_b_to_mate(HEADS - 1, 0)
-    pl.loop(1, HEADS)(lambda e: pass_a(e, 0))
+    pl.loop(0, HEADS)(lambda e: end_a(e, 0))
 
     width = HEADS * n_b
     span = K * n_a
-    pl.loop(0, HEADS)(lambda e: end_b(e, 0))
-
-    @pl.loop(0, 2 * Q)
-    def _(r):
-        keys_t[r] = in_b[r, :, 0].reshape(width, HEAD).T
-
     def rows_at(e):
         return pl.ds(pl.multiple_of(head_at(e) * span, span), span)
 
     def lane_groups(x):
         return [x[:, j:j + HEAD] for j in range(0, width, HEAD)]
 
-    def score_block(e):
-        queries = in_a[head_at(e), :, 0].reshape(span, HEAD)
-        peak = jnp.full((span, HEAD), -jnp.inf, jnp.float32)
-        for r in range(2 * Q):
-            logits = jnp.dot(queries, keys_t[r], preferred_element_type=jnp.float32) * to_log2
-            scores[r, rows_at(e), :] = logits
-            tops = jnp.max(logits.reshape(span // 8, 8, width), axis=0)
-            peak_b[r] = jnp.maximum(peak_b[r], tops)
-            peak = functools.reduce(jnp.maximum, lane_groups(logits), peak)
-        peak_a[e] = peak
-
-    @pl.loop(0, HEADS)
-    def _(e):
-        end_a(e, 0)
-        score_block(e)
-
-        @pl.when(e > 0)
-        def _():
-            pass_a(e, 1)
+    def score_block(r):
+        keys_t = in_b[r, :, 0].reshape(width, HEAD).T
+        tops = jnp.full((8, width), -jnp.inf, jnp.float32)
+        for h in range(HEADS):
+            queries = in_a[h, :, 0].reshape(span, HEAD)
+            logits = jnp.dot(queries, keys_t, preferred_element_type=jnp.float32) * to_log2
+            scores[r, h * span:(h + 1) * span, :] = logits
+            tops = jnp.maximum(tops, jnp.max(logits.reshape(span // 8, 8, width), axis=0))
+            peak_a[h] = functools.reduce(jnp.maximum, lane_groups(logits), peak_a[h])
+        peak_b[r] = tops
+
+    @pl.loop(0, 2 * Q)
+    def _(t):
+        @pl.when(t == 1)
+        def _():
+            pass_b_to_mate(HEADS - 1, 0)
+
+        near = t < Q
+        r = lax.rem(q + lax.rem(t, Q), Q) * 2 + jnp.where(near, c, 1 - c)
+
+        @pl.when(t >= Q)
+        def _():
+            pl.loop(0, HEADS)(lambda e: wait_b(r, e, 0, mate))
+
+        score_block(r)
+
+        @pl.when((t > 0) & (t < HEADS))
+        def _():
+            pass_a(t, 1)
+
+    for e in range(2 * Q, HEADS):
+        pass_a(e, 1)
 
     def row_block(e):
         pp = head_at(e)
-        peak = jnp.max(peak_a[e], axis=1, keepdims=True)
+        peak = jnp.max(peak_a[pp], axis=1, keepdims=True)
         totals = jnp.zeros((span, HEAD), jnp.float32)
         num = jnp.zeros((span, HEAD), jnp.float32)
         for r in range(2 * Q):
@@ -306,28 +314,28 @@
     def done_copy(e, done, back, send, recv):
         return remote(done.at[head_at(e)], back.at[p], send.at[e], recv.at[p], at_head(e))
 
-    def take_done(e, done, back, out, send, recv):
+    def wait_done(e, done, back, send, recv):
         h = head_at(e)
         remote(done.at[h], back.at[h], send.at[e], recv.at[h], at_head(e)).wait_recv()
-        n = out.shape[0]
-        scale = back[h, n:n + EXTRA].astype(jnp.float32)[0:1]
-        out[:, head_lanes(h)] = value_of(back[h, 0:n], scale)
-
-    def finish(e, parts, done, back, out, send, recv):
+
+    def finish(e, parts, done, back, send, recv):
         num, total, _ = merged(parts)
         result = (num / total).T
+        n = result.shape[0]
+        scale = scale_of(result)
+        codes = code_of(result, scale.astype(jnp.float32))
+        extra = jnp.broadcast_to(scale, (EXTRA, HEAD))
 
         @pl.when(e > 0)
         def _():
-            n = out.shape[0]
-            scale = scale_of(result)
-            done[head_at(e), 0:n] = code_of(result, scale.astype(jnp.float32))
-            done[head_at(e), n:n + EXTRA] = jnp.broadcast_to(scale, (EXTRA, HEAD))
+            done[head_at(e), 0:n] = codes
+            done[head_at(e), n:n + EXTRA] = extra
             done_copy(e, done, back, send, recv).start()
 
         @pl.when(e == 0)
         def _():
-            out[:, own_lanes] = result
+            back[p, 0:n] = codes
+            back[p, n:n + EXTRA] = extra
 
     def finish_a(e):
         h = head_at(e)
@@ -339,7 +347,7 @@
                 at_k(d),
             ).wait_recv()
             parts.append(sent_part_of(got_a.at[kk, h]))
-        finish(e, parts, done_a, back_a, out_a, done_a_send, done_a_recv)
+        finish(e, parts, done_a, back_a, done_a_send, done_a_recv)
 
     def finish_b(e):
         h = head_at(e)
@@ -351,7 +359,7 @@
                 got_b_recv.at[qq, h], at_q(d),
             ).wait_recv()
             parts.append(sent_part_of(got_b.at[qq, h]))
-        finish(e, parts, done_b, back_b, out_b, done_b_send, done_b_recv)
+        finish(e, parts, done_b, back_b, done_b_send, done_b_recv)
 
     def merge_mate(d):
         qq = lax.rem(q + d, Q)
@@ -415,11 +423,8 @@
 
     @pl.loop(1, HEADS)
     def _(e):
-        take_done(e, done_b, back_b, out_b, done_b_send, done_b_recv)
-
-    @pl.loop(1, HEADS)
-    def _(e):
-        take_done(e, done_a, back_a, out_a, done_a_send, done_a_recv)
+        wait_done(e, done_b, back_b, done_b_send, done_b_recv)
+        wait_done(e, done_a, back_a, done_a_send, done_a_recv)
 
     @pl.loop(1, HEADS)
     def _(e):
@@ -446,6 +451,14 @@
     pl.loop(0, Q)(lambda d: mate_b_copy(d).wait_send())
 
 
+def decode(back_a, back_b, out_a, out_b):
+    for back, out in ((back_a, out_a), (back_b, out_b)):
+        n = out.shape[0]
+        for h in range(HEADS):
+            scale = back[h, n:n + EXTRA].astype(jnp.float32)[0:1]
+            out[:, h * HEAD:(h + 1) * HEAD] = value_of(back[h, 0:n], scale)
+
+
 def on_device(rows, cols, rep_a, val_a, rep_b, val_b):
     Q, K = rows // HEADS, cols // 2
     n_a, n_b = rep_a.shape[0], rep_b.shape[0]
@@ -455,18 +468,17 @@
     vmem = pl.BlockSpec(memory_space=pltpu.VMEM)
     hbm = pl.BlockSpec(memory_space=pltpu.HBM)
     tile = K * HEADS * n_a * 2 * Q * HEADS * n_b
-    return pl.pallas_call(
+    back_a, back_b = pl.pallas_call(
         functools.partial(kernel, rows, cols),
         out_shape=(
-            jax.ShapeDtypeStruct(rep_a.shape, f32),
-            jax.ShapeDtypeStruct(rep_b.shape, f32),
+            jax.ShapeDtypeStruct((HEADS, n_a + EXTRA, HEAD), bf16),
+            jax.ShapeDtypeStruct((HEADS, n_b + EXTRA, HEAD), bf16),
         ),
         in_specs=[hbm] * 4,
         out_specs=(vmem, vmem),
         scratch_shapes=[
             pltpu.VMEM((HEADS, K, 2, n_a, HEAD), bf16),
             pltpu.VMEM((2 * Q, HEADS, 2, n_b, HEAD), bf16),
-            pltpu.VMEM((2 * Q, HEAD, HEADS * n_b), bf16),
             pltpu.VMEM((HEAD, HEADS * K * n_a), bf16),
             pltpu.VMEM((2 * Q, K * HEADS * n_a, HEADS * n_b), f32),
             pltpu.VMEM((HEADS, K * n_a, HEAD), f32),
@@ -480,8 +492,6 @@
             pltpu.VMEM((Q, HEADS, HEAD + EXTRA, n_b), bf16),
             pltpu.VMEM((HEADS, n_a + EXTRA, HEAD), bf16),
             pltpu.VMEM((HEADS, n_b + EXTRA, HEAD), bf16),
-            pltpu.VMEM((HEADS, n_a + EXTRA, HEAD), bf16),
-            pltpu.VMEM((HEADS, n_b + EXTRA, HEAD), bf16),
             dma((4,)), dma((HEADS, 2)), dma((HEADS, 2)),
             dma((K, HEADS, 2)), dma((2 * Q, HEADS, 2)),
             dma((K, HEADS, 2)), dma((Q, HEADS, 2)), dma((Q, HEADS, 2)),
@@ -491,12 +501,22 @@
             dma((HEADS,)), dma((HEADS,)), dma((HEADS,)), dma((HEADS,)),
         ],
         compiler_params=pltpu.CompilerParams(
-            collective_id=0, has_side_effects=True, vmem_limit_bytes=127 * 512 * 1024
+            collective_id=0, has_side_effects=True, vmem_limit_bytes=GRANT
         ),
         cost_estimate=pl.CostEstimate(
             flops=6 * tile * HEAD, bytes_accessed=6 * 1024 * (n_a + n_b), transcendentals=2 * tile
         ),
     )(rep_a, val_a, rep_b, val_b)
+    return pl.pallas_call(
+        decode,
+        out_shape=(
+            jax.ShapeDtypeStruct(rep_a.shape, f32),
+            jax.ShapeDtypeStruct(rep_b.shape, f32),
+        ),
+        in_specs=[vmem] * 2,
+        out_specs=(vmem, vmem),
+        compiler_params=pltpu.CompilerParams(vmem_limit_bytes=GRANT),
+    )(back_a, back_b)
 
 
 def solution(mesh):

time: 48 us -> 48.2 us (level)
  Pallas kernels: 44.7 us -> 47.4 us
  local copies, waits for them, and re-layouts: 2.42 us -> 0 us
    unnamed x4 -> x0, local copies, waits for them, and re-layouts: 2.42 us -> none
    pallas_call x0 -> x1, Pallas kernels: none -> 1.87 us  [on_device(): pl.pallas_call(decode, out_shape=(jax.ShapeDtypeStruct(rep_a.shape, f32),...]
    pallas_call x1, Pallas kernels: 44.7 us -> 45.5 us  [on_device(): pl.pallas_call(functools.partial(kernel, rows, cols), out_shape=(jax.Shap...]
where the time goes in v6:
time: 48.2 us; the launch traced here: 48 us
  Pallas kernels  47.4 us (98%)
  between operations  0.64 us (1%)
    pallas_call x1, Pallas kernels, on_device(): pl.pallas_call(functools.partial(kernel, rows, cols), out_shape=(jax.Shap...  45.5 us
    pallas_call x1, Pallas kernels, on_device(): pl.pallas_call(decode, out_shape=(jax.ShapeDtypeStruct(rep_a.shape, f32),...  1.87 us

profile of v6, /device:TPU:0, one launch (start us, length us, event | category | flops | bytes accessed | tf_op | source)
XLA Modules:
  0.0 48.0 jit_solution(5030923826283366138)
XLA Ops:
  0.6 45.5 %shard_map.59 = (bf16[4,144,128]{2,1,0:T(8,128)(2,1)}, bf16[4,144,128]{2,1,0:T(8,128)(2,1)}) custom-call(bf16[128,512]{1,0:T(8,128)(2,1)} %rep_a.1, bf16[128,512]{1,0:T(8,128)(2,1)} %val_a.1, bf16[128,512]{1,0:T(8,128)(2,1)} %rep_b.1, bf16[128,512]{1,0:T(8,128)(2,1)} %val_b.1), custom_call_target="tpu_custom_call" | custom-call | flops 1610612736 | bytes 1572864 | tf_op jit(solution)/shard_map/pallas_call | solution.py:471
  46.1 1.9 %shard_map.60 = (f32[128,512]{1,0:T(8,128)}, f32[128,512]{1,0:T(8,128)}) custom-call(bf16[4,144,128]{2,1,0:T(8,128)(2,1)} %get-tuple-element.4.back_a, bf16[4,144,128]{2,1,0:T(8,128)(2,1)} %get-tuple-element.5.back_b), custom_call_target="tpu_custom_call" | custom-call | tf_op jit(solution)/shard_map/pallas_call | solution.py:510

commit v7 on v6

--- a/solution.py
+++ b/solution.py
@@ -73,7 +73,7 @@
     rep_a, val_a, rep_b, val_b, back_a, back_b,
     in_a, in_b, values_t, scores, peak_a, peak_b,
     part_a, code_a, got_a, part_b, mate_b, code_b, got_b, done_a, done_b,
-    own, cut_a_send, cut_b_send, a_recv, b_recv, a_send, b_send, mate_send,
+    own, cut_a_send, cut_b_send, a_recv, b_recv, a_all, b_all, a_send, b_send, mate_send,
     part_a_send, got_a_recv, mate_b_send, mate_b_recv, part_b_send, got_b_recv,
     done_a_send, done_b_send, done_a_recv, done_b_recv,
 ):
@@ -140,55 +140,51 @@
         )
 
     def a_copy(d, e, i):
-        h = head_at(e)
-        piece = in_a.at[h, k, i]
-        return remote(piece, piece, a_send.at[d, e, i], a_recv.at[k, h, i], at_k(d))
+        piece = in_a.at[head_at(e), k, i]
+        return remote(piece, piece, a_send.at[d, e, i], a_all.at[k, i], at_k(d))
 
     def b_copy(d, e, i):
-        h = head_at(e)
-        piece = in_b.at[s, h, i]
-        return remote(piece, piece, b_send.at[d, e, i], b_recv.at[s, h, i], at_q(d))
-
-    def mate_copy(d, e, i):
-        r, h = lax.rem(q + d, Q) * 2 + c, head_at(e)
-        piece = in_b.at[r, h, i]
-        return remote(piece, piece, mate_send.at[d, e, i], b_recv.at[r, h, i], mate)
-
-    def wait_b(r, e, i, device):
-        h = head_at(e)
-        piece = in_b.at[r, h, i]
-        remote(piece, piece, mate_send.at[0, 0, i], b_recv.at[r, h, i], device).wait_recv()
-
-    def wait_a(r, e, i, device):
-        h = head_at(e)
-        piece = in_a.at[h, r, i]
-        remote(piece, piece, mate_send.at[0, 0, i], a_recv.at[r, h, i], device).wait_recv()
+        piece = in_b.at[s, head_at(e), i]
+        return remote(piece, piece, b_send.at[d, e, i], b_all.at[s, i], at_q(d))
+
+    def mate_copy(d, i):
+        r = lax.rem(q + d, Q) * 2 + c
+        block = in_b.at[r, :, i]
+        return remote(block, block, mate_send.at[d, i], b_all.at[r, i], mate)
 
     def pass_b(e, i, own=False):
         if not own:
-            wait_b(s, e, i, at_head(e))
+            piece = in_b.at[s, head_at(e), i]
+            remote(
+                piece, piece, cut_b_send.at[e, i], b_recv.at[s, head_at(e), i], at_head(e)
+            ).wait_recv()
         for d in range(1, Q):
             b_copy(d, e, i).start()
-        mate_copy(0, e, i).start()
-
-    def pass_b_to_mate(e, i):
+
+    def wait_b(r, i, device):
+        block = in_b.at[r, :, i]
+        remote(block, block, mate_send.at[0, i], b_all.at[r, i], device).wait_recv()
+
+    def pass_b_to_mate(i):
         for d in range(1, Q):
-            wait_b(lax.rem(q + d, Q) * 2 + c, e, i, at_q(d))
-            mate_copy(d, e, i).start()
-
-    def end_b(e, i):
-        for d in range(Q):
-            wait_b(lax.rem(q + d, Q) * 2 + 1 - c, e, i, mate)
+            wait_b(lax.rem(q + d, Q) * 2 + c, i, at_q(d))
+            mate_copy(d, i).start()
 
     def pass_a(e, i, own=False):
         if not own:
-            wait_a(k, e, i, at_head(e))
+            piece = in_a.at[head_at(e), k, i]
+            remote(
+                piece, piece, cut_a_send.at[e, i], a_recv.at[k, head_at(e), i], at_head(e)
+            ).wait_recv()
         for d in range(1, K):
             a_copy(d, e, i).start()
 
-    def end_a(e, i):
+    def end_a(i):
         for d in range(1, K):
-            wait_a(lax.rem(k + d, K), e, i, at_k(d))
+            block = in_a.at[:, lax.rem(k + d, K), i]
+            remote(
+                block, block, a_send.at[d, 0, i], a_all.at[lax.rem(k + d, K), i], at_k(d)
+            ).wait_recv()
 
     for cut, i in ((cut_a_copy, 0), (cut_b_copy, 0), (cut_a_copy, 1), (cut_b_copy, 1)):
         pl.loop(1, HEADS)(lambda d, cut=cut, i=i: cut(d, i).start())
@@ -199,12 +195,9 @@
         pass_b(0, i, own=True)
     pl.loop(1, HEADS)(lambda e: pass_a(e, 0))
 
-    @pl.loop(1, HEADS)
-    def _(e):
-        pass_b(e, 0)
-        pass_b_to_mate(e - 1, 0)
-
-    pl.loop(0, HEADS)(lambda e: end_a(e, 0))
+    pl.loop(1, HEADS)(lambda e: pass_b(e, 0))
+    mate_copy(0, 0).start()
+    end_a(0)
 
     width = HEADS * n_b
     span = K * n_a
@@ -229,14 +222,14 @@
     def _(t):
         @pl.when(t == 1)
         def _():
-            pass_b_to_mate(HEADS - 1, 0)
+            pass_b_to_mate(0)
 
         near = t < Q
         r = lax.rem(q + lax.rem(t, Q), Q) * 2 + jnp.where(near, c, 1 - c)
 
         @pl.when(t >= Q)
         def _():
-            pl.loop(0, HEADS)(lambda e: wait_b(r, e, 0, mate))
+            wait_b(r, 0, mate)
 
         score_block(r)
 
@@ -279,7 +272,7 @@
             code_a.at[there, h], got_a.at[k, h], part_a_send.at[d, e], got_a_recv.at[k, h], at_k(d)
         )
 
-    pl.loop(0, HEADS)(lambda e: end_a(e, 1))
+    end_a(1)
     values_t[...] = in_a[:, :, 1].reshape(HEADS * span, HEAD).T
 
     def col_block(r):
@@ -396,16 +389,18 @@
         @pl.when(t == 0)
         def _():
             pl.loop(1, HEADS)(lambda e: pass_b(e, 1))
+            mate_copy(0, 1).start()
 
         @pl.when(t == Q - 1)
         def _():
-            pl.loop(0, HEADS)(lambda e: pass_b_to_mate(e, 1))
+            pass_b_to_mate(1)
 
         @pl.when(t >= Q)
         def _():
             merge_mate(d)
 
-    pl.loop(0, HEADS)(lambda e: end_b(e, 1))
+    for d in range(Q):
+        wait_b(lax.rem(q + d, Q) * 2 + 1 - c, 1, mate)
 
     @pl.loop(0, HEADS + 1)
     def _(n):
@@ -415,24 +410,17 @@
             row_block(e)
             for d in range(1, K):
                 part_a_copy(d, e).start()
-            finish_b(e)
 
         @pl.when(n > 0)
         def _():
+            finish_b(lax.rem(n, HEADS))
             finish_a(lax.rem(n, HEADS))
-
-    @pl.loop(1, HEADS)
-    def _(e):
-        wait_done(e, done_b, back_b, done_b_send, done_b_recv)
-        wait_done(e, done_a, back_a, done_a_send, done_a_recv)
 
     @pl.loop(1, HEADS)
     def _(e):
         for i in range(2):
             cut_b_copy(e, i).wait_send()
             cut_a_copy(e, i).wait_send()
-        done_copy(e, done_a, back_a, done_a_send, done_a_recv).wait_send()
-        done_copy(e, done_b, back_b, done_b_send, done_b_recv).wait_send()
 
     @pl.loop(0, HEADS)
     def _(e):
@@ -440,15 +428,22 @@
             for i in range(2):
                 a_copy(d, e, i).wait_send()
             part_a_copy(d, e).wait_send()
-        for d in range(Q):
+        for d in range(1, Q):
             for i in range(2):
-                if d:
-                    b_copy(d, e, i).wait_send()
-                mate_copy(d, e, i).wait_send()
-            if d:
-                part_b_copy(d, e).wait_send()
-
-    pl.loop(0, Q)(lambda d: mate_b_copy(d).wait_send())
+                b_copy(d, e, i).wait_send()
+            part_b_copy(d, e).wait_send()
+
+    for d in range(Q):
+        for i in range(2):
+            mate_copy(d, i).wait_send()
+        mate_b_copy(d).wait_send()
+
+    @pl.loop(1, HEADS)
+    def _(e):
+        done_copy(e, done_a, back_a, done_a_send, done_a_recv).wait_send()
+        done_copy(e, done_b, back_b, done_b_send, done_b_recv).wait_send()
+        wait_done(e, done_b, back_b, done_b_send, done_b_recv)
+        wait_done(e, done_a, back_a, done_a_send, done_a_recv)
 
 
 def decode(back_a, back_b, out_a, out_b):
@@ -494,7 +489,8 @@
             pltpu.VMEM((HEADS, n_b + EXTRA, HEAD), bf16),
             dma((4,)), dma((HEADS, 2)), dma((HEADS, 2)),
             dma((K, HEADS, 2)), dma((2 * Q, HEADS, 2)),
-            dma((K, HEADS, 2)), dma((Q, HEADS, 2)), dma((Q, HEADS, 2)),
+            dma((K, 2)), dma((2 * Q, 2)),
+            dma((K, HEADS, 2)), dma((Q, HEADS, 2)), dma((Q, 2)),
             dma((K, HEADS)), dma((K, HEADS)),
             dma((Q,)), dma((Q,)),
             dma((Q, HEADS)), dma((Q, HEADS)),

time: 48.2 us -> 46.1 us (0.956)
  Pallas kernels: 47.4 us -> 45.3 us
    pallas_call x1, Pallas kernels: 45.5 us -> 43.5 us  [on_device(): pl.pallas_call(functools.partial(kernel, rows, cols), out_shape=(jax.Shap...]
where the time goes in v7:
time: 46.1 us; the launch traced here: 46 us
  Pallas kernels  45.3 us (98%)
  between operations  0.64 us (1%)
    pallas_call x1, Pallas kernels, on_device(): pl.pallas_call(functools.partial(kernel, rows, cols), out_shape=(jax.Shap...  43.5 us
    pallas_call x1, Pallas kernels, on_device(): pl.pallas_call(decode, out_shape=(jax.ShapeDtypeStruct(rep_a.shape, f32),...  1.87 us

profile of v7, /device:TPU:0, one launch (start us, length us, event | category | flops | bytes accessed | tf_op | source)
XLA Modules:
  0.0 46.0 jit_solution(16911956303579203907)
XLA Ops:
  0.6 43.5 %shard_map.59 = (bf16[4,144,128]{2,1,0:T(8,128)(2,1)}, bf16[4,144,128]{2,1,0:T(8,128)(2,1)}) custom-call(bf16[128,512]{1,0:T(8,128)(2,1)} %rep_a.1, bf16[128,512]{1,0:T(8,128)(2,1)} %val_a.1, bf16[128,512]{1,0:T(8,128)(2,1)} %rep_b.1, bf16[128,512]{1,0:T(8,128)(2,1)} %val_b.1), custom_call_target="tpu_custom_call" | custom-call | flops 1610612736 | bytes 1572864 | tf_op jit(solution)/shard_map/pallas_call | solution.py:466
  44.1 1.9 %shard_map.60 = (f32[128,512]{1,0:T(8,128)}, f32[128,512]{1,0:T(8,128)}) custom-call(bf16[4,144,128]{2,1,0:T(8,128)(2,1)} %get-tuple-element.4.back_a, bf16[4,144,128]{2,1,0:T(8,128)(2,1)} %get-tuple-element.5.back_b), custom_call_target="tpu_custom_call" | custom-call | tf_op jit(solution)/shard_map/pallas_call | solution.py:506

commit v8 on v7

--- a/solution.py
+++ b/solution.py
@@ -186,17 +186,19 @@
                 block, block, a_send.at[d, 0, i], a_all.at[lax.rem(k + d, K), i], at_k(d)
             ).wait_recv()
 
-    for cut, i in ((cut_a_copy, 0), (cut_b_copy, 0), (cut_a_copy, 1), (cut_b_copy, 1)):
-        pl.loop(1, HEADS)(lambda d, cut=cut, i=i: cut(d, i).start())
+    pl.loop(1, HEADS)(lambda d: cut_a_copy(d, 0).start())
+    pl.loop(1, HEADS)(lambda d: cut_b_copy(d, 0).start())
     for copy in own_copies:
         copy.wait()
-    for i in range(2):
-        pass_a(0, i, own=True)
-        pass_b(0, i, own=True)
+    pass_a(0, 0, own=True)
+    pass_b(0, 0, own=True)
     pl.loop(1, HEADS)(lambda e: pass_a(e, 0))
-
+    pl.loop(1, HEADS)(lambda d: cut_a_copy(d, 1).start())
     pl.loop(1, HEADS)(lambda e: pass_b(e, 0))
+    pl.loop(1, HEADS)(lambda d: cut_b_copy(d, 1).start())
     mate_copy(0, 0).start()
+    pass_a(0, 1, own=True)
+    pass_b(0, 1, own=True)
     end_a(0)
 
     width = HEADS * n_b

time: 46.1 us -> 43.8 us (0.950)
  Pallas kernels: 45.3 us -> 43 us
    pallas_call x1, Pallas kernels: 43.5 us -> 41.1 us  [on_device(): pl.pallas_call(functools.partial(kernel, rows, cols), out_shape=(jax.Shap...]
where the time goes in v8:
time: 43.8 us; the launch traced here: 43.6 us
  Pallas kernels  43 us (98%)
  between operations  0.64 us (1%)
    pallas_call x1, Pallas kernels, on_device(): pl.pallas_call(functools.partial(kernel, rows, cols), out_shape=(jax.Shap...  41.1 us
    pallas_call x1, Pallas kernels, on_device(): pl.pallas_call(decode, out_shape=(jax.ShapeDtypeStruct(rep_a.shape, f32),...  1.87 us

profile of v8, /device:TPU:0, one launch (start us, length us, event | category | flops | bytes accessed | tf_op | source)
XLA Modules:
  0.0 43.6 jit_solution(10158280260409878272)
XLA Ops:
  0.6 41.1 %shard_map.59 = (bf16[4,144,128]{2,1,0:T(8,128)(2,1)}, bf16[4,144,128]{2,1,0:T(8,128)(2,1)}) custom-call(bf16[128,512]{1,0:T(8,128)(2,1)} %rep_a.1, bf16[128,512]{1,0:T(8,128)(2,1)} %val_a.1, bf16[128,512]{1,0:T(8,128)(2,1)} %rep_b.1, bf16[128,512]{1,0:T(8,128)(2,1)} %val_b.1), custom_call_target="tpu_custom_call" | custom-call | flops 1610612736 | bytes 1572864 | tf_op jit(solution)/shard_map/pallas_call | solution.py:468
  41.7 1.9 %shard_map.60 = (f32[128,512]{1,0:T(8,128)}, f32[128,512]{1,0:T(8,128)}) custom-call(bf16[4,144,128]{2,1,0:T(8,128)(2,1)} %get-tuple-element.4.back_a, bf16[4,144,128]{2,1,0:T(8,128)(2,1)} %get-tuple-element.5.back_b), custom_call_target="tpu_custom_call" | custom-call | tf_op jit(solution)/shard_map/pallas_call | solution.py:508

commit v9 on v8

--- a/solution.py
+++ b/solution.py
@@ -235,12 +235,9 @@
 
         score_block(r)
 
-        @pl.when((t > 0) & (t < HEADS))
-        def _():
-            pass_a(t, 1)
-
-    for e in range(2 * Q, HEADS):
-        pass_a(e, 1)
+        @pl.when(t == 2 * Q - 2)
+        def _():
+            pl.loop(1, HEADS)(lambda e: pass_a(e, 1))
 
     def row_block(e):
         pp = head_at(e)
@@ -393,7 +390,7 @@
             pl.loop(1, HEADS)(lambda e: pass_b(e, 1))
             mate_copy(0, 1).start()
 
-        @pl.when(t == Q - 1)
+        @pl.when(t == Q)
         def _():
             pass_b_to_mate(1)
 

time: 43.8 us -> 42.8 us (0.977)
  Pallas kernels: 43 us -> 42 us
    pallas_call x1, Pallas kernels: 41.1 us -> 40.1 us  [on_device(): pl.pallas_call(functools.partial(kernel, rows, cols), out_shape=(jax.Shap...]
where the time goes in v9:
time: 42.8 us; the launch traced here: 42.6 us
  Pallas kernels  42 us (98%)
  between operations  0.64 us (1%)
    pallas_call x1, Pallas kernels, on_device(): pl.pallas_call(functools.partial(kernel, rows, cols), out_shape=(jax.Shap...  40.1 us
    pallas_call x1, Pallas kernels, on_device(): pl.pallas_call(decode, out_shape=(jax.ShapeDtypeStruct(rep_a.shape, f32),...  1.87 us

profile of v9, /device:TPU:0, one launch (start us, length us, event | category | flops | bytes accessed | tf_op | source)
XLA Modules:
  0.0 42.6 jit_solution(1060539370142108546)
XLA Ops:
  0.6 40.1 %shard_map.59 = (bf16[4,144,128]{2,1,0:T(8,128)(2,1)}, bf16[4,144,128]{2,1,0:T(8,128)(2,1)}) custom-call(bf16[128,512]{1,0:T(8,128)(2,1)} %rep_a.1, bf16[128,512]{1,0:T(8,128)(2,1)} %val_a.1, bf16[128,512]{1,0:T(8,128)(2,1)} %rep_b.1, bf16[128,512]{1,0:T(8,128)(2,1)} %val_b.1), custom_call_target="tpu_custom_call" | custom-call | flops 1610612736 | bytes 1572864 | tf_op jit(solution)/shard_map/pallas_call | solution.py:465
  40.8 1.9 %shard_map.60 = (f32[128,512]{1,0:T(8,128)}, f32[128,512]{1,0:T(8,128)}) custom-call(bf16[4,144,128]{2,1,0:T(8,128)(2,1)} %get-tuple-element.4.back_a, bf16[4,144,128]{2,1,0:T(8,128)(2,1)} %get-tuple-element.5.back_b), custom_call_target="tpu_custom_call" | custom-call | tf_op jit(solution)/shard_map/pallas_call | solution.py:505

commit v10 on v9

--- a/solution.py
+++ b/solution.py
@@ -187,14 +187,16 @@
             ).wait_recv()
 
     pl.loop(1, HEADS)(lambda d: cut_a_copy(d, 0).start())
-    pl.loop(1, HEADS)(lambda d: cut_b_copy(d, 0).start())
     for copy in own_copies:
         copy.wait()
     pass_a(0, 0, own=True)
     pass_b(0, 0, own=True)
-    pl.loop(1, HEADS)(lambda e: pass_a(e, 0))
+    pass_a(1, 0)
+    pl.loop(1, HEADS)(lambda d: cut_b_copy(d, 0).start())
+    pl.loop(2, HEADS)(lambda e: pass_a(e, 0))
+    pass_b(1, 0)
     pl.loop(1, HEADS)(lambda d: cut_a_copy(d, 1).start())
-    pl.loop(1, HEADS)(lambda e: pass_b(e, 0))
+    pl.loop(2, HEADS)(lambda e: pass_b(e, 0))
     pl.loop(1, HEADS)(lambda d: cut_b_copy(d, 1).start())
     mate_copy(0, 0).start()
     pass_a(0, 1, own=True)

time: 42.8 us -> 44.7 us (1.044)
  Pallas kernels: 42 us -> 43.9 us
    pallas_call x1, Pallas kernels: 40.1 us -> 42 us  [on_device(): pl.pallas_call(functools.partial(kernel, rows, cols), out_shape=(jax.Shap...]
where the time goes in v10:
time: 44.7 us; the launch traced here: 44.5 us
  Pallas kernels  43.9 us (98%)
  between operations  0.64 us (1%)
    pallas_call x1, Pallas kernels, on_device(): pl.pallas_call(functools.partial(kernel, rows, cols), out_shape=(jax.Shap...  42 us
    pallas_call x1, Pallas kernels, on_device(): pl.pallas_call(decode, out_shape=(jax.ShapeDtypeStruct(rep_a.shape, f32),...  1.87 us

profile of v10, /device:TPU:0, one launch (start us, length us, event | category | flops | bytes accessed | tf_op | source)
XLA Modules:
  0.0 44.5 jit_solution(2274953021704913921)
XLA Ops:
  0.6 42.0 %shard_map.59 = (bf16[4,144,128]{2,1,0:T(8,128)(2,1)}, bf16[4,144,128]{2,1,0:T(8,128)(2,1)}) custom-call(bf16[128,512]{1,0:T(8,128)(2,1)} %rep_a.1, bf16[128,512]{1,0:T(8,128)(2,1)} %val_a.1, bf16[128,512]{1,0:T(8,128)(2,1)} %rep_b.1, bf16[128,512]{1,0:T(8,128)(2,1)} %val_b.1), custom_call_target="tpu_custom_call" | custom-call | flops 1610612736 | bytes 1572864 | tf_op jit(solution)/shard_map/pallas_call | solution.py:467
  42.6 1.9 %shard_map.60 = (f32[128,512]{1,0:T(8,128)}, f32[128,512]{1,0:T(8,128)}) custom-call(bf16[4,144,128]{2,1,0:T(8,128)(2,1)} %get-tuple-element.4.back_a, bf16[4,144,128]{2,1,0:T(8,128)(2,1)} %get-tuple-element.5.back_b), custom_call_target="tpu_custom_call" | custom-call | tf_op jit(solution)/shard_map/pallas_call | solution.py:507
